TPU v7x, 256 devices: a whole 4x4x8 slice. The times are simulated.
256 devices in a mesh: in: 8 (over z), out: 4 (over y_hi, core), dep: 8 (over x, y_lo).
Axes of the slice: x: 4, y: 4 (y_hi: 2, y_lo: 2; y = y_hi * 2 + y_lo), z: 8, core: 2. Of those that a mesh axis runs over, the one named last changes fastest.
Arguments:
- tokens: bfloat16 [8, 512, 3072], P('dep', 'in', 'out'), may hold values from -48 to 48
- norm_gain: float32 [3072], P('out'), may hold values from 0.1 to 1.9
- qkv_weight: bfloat16 [3072, 3, 3072], P(('out', 'dep'), None, 'in'), may hold values from -0.109375 to 0.109375
- head_gain: float32 [2, 128], replicated, may hold values from 1 to 5, as said below
- out_weight: bfloat16 [3072, 3072], P(('in', 'dep'), 'out'), may hold values from -0.109375 to 0.109375
- up_weight: bfloat16 [3072, 12288], P(('out', 'dep'), 'in'), may hold values from -0.109375 to 0.109375
- down_weight: bfloat16 [12288, 3072], P(('in', 'dep'), 'out'), may hold values from -0.0546875 to 0.0546875
- upstream: bfloat16 [8, 512, 3072], P('dep', 'in', 'out'), may hold values from -6 to 6
Outputs:
- layer_out: bfloat16 [8, 512, 3072], P('dep', 'in', 'out')
- token_grad: bfloat16 [8, 512, 3072], P('dep', 'in', 'out')
- norm_gain_grad: float32 [3072], P('out')
- head_gain_grad: float32 [2, 128], replicated
- qkv_weight_grad: float32 [3072, 3, 3072], P(('out', 'dep'), None, 'in')
- out_weight_grad: float32 [3072, 3072], P(('in', 'dep'), 'out')
- up_weight_grad: float32 [3072, 12288], P(('out', 'dep'), 'in')
- down_weight_grad: float32 [12288, 3072], P(('in', 'dep'), 'out')
Inputs may be any that keep to these rules, and one draw needn't show every extreme that they name: `head_gain`: every entry is positive.
All inputs are finite; a program needn't handle non-finite values.
Results may differ from a plain program's by a relative error of at most 0.02.
The roundings to bfloat16 on the way count: a program that leaves them out, or rounds other values in their place, can miss the bound.
Values may be sent and summed in bfloat16 or wider, within the bound.
A program may use at most 128 MiB of HBM per device.

v0:
```python
import math

import jax
import jax.numpy as jnp
from jax import lax
from jax.sharding import PartitionSpec as P

HEAD_DIM = 128


EPSILON = 1e-06
ROOT_HALF = 1.0 / math.sqrt(2.0)
ROOT_TWO_PI = math.sqrt(2.0 * math.pi)


def normalize(values):
    average = jnp.mean(values, axis=-1, keepdims=True)
    spread = jnp.mean(values * values, axis=-1, keepdims=True) - average * average
    inverse = lax.rsqrt(spread + EPSILON)
    return ((values - average) * inverse, inverse)


def normalize_back(incoming, normed, inverse):
    first = jnp.mean(incoming, axis=-1, keepdims=True)
    second = jnp.mean(incoming * normed, axis=-1, keepdims=True)
    return inverse * (incoming - first - normed * second)


def gelu_pair(values):
    below = 0.5 * (1.0 + jax.scipy.special.erf(values * ROOT_HALF))
    slope = below + values * jnp.exp(-0.5 * values * values) / ROOT_TWO_PI
    return (values * below, slope)


def row_totals(first, second):
    return lax.psum((jnp.sum(first, axis=1), jnp.sum(second, axis=1)), "out")


def group_gather(values):
    return lax.all_gather(values, "in", axis=0, tiled=True)


def head_gather(first, second):
    return (
        lax.all_gather(first, "out", axis=0, tiled=True),
        lax.all_gather(second, "out", axis=0, tiled=True),
    )


def token_reduce(term, rows):
    return lax.psum_scatter(
        term(jnp.int32(0), rows * lax.axis_size("out")), "out", scatter_dimension=0, tiled=True
    )


def feature_reduce(term, rows):
    return lax.psum_scatter(
        term(jnp.int32(0), rows * lax.axis_size("in")), "in", scatter_dimension=0, tiled=True
    )


def body(tokens, norm_gain, qkv_weight, head_gain, out_weight, up_weight, down_weight, upstream):
    width = tokens.shape[2] * lax.axis_size("out")
    local_rows = tokens.shape[1]
    attn_here = qkv_weight.shape[2]
    heads_here = attn_here // HEAD_DIM
    scale = HEAD_DIM ** (-0.5)
    wide = tokens[0].astype(jnp.float32)
    summed, squares = row_totals(wide, wide * wide)
    average = summed / width
    spread = squares / width - average * average
    inverse = lax.rsqrt(spread + EPSILON)
    normed = (wide - average[:, None]) * inverse[:, None]
    hidden_in = (normed * norm_gain).astype(jnp.bfloat16)
    group_in = group_gather(hidden_in)
    group_count = group_in.shape[0]
    own_rows = group_count // lax.axis_size("out")
    qkv_all, up_all = (
        lax.all_gather(qkv_weight, "dep", axis=0, tiled=True),
        lax.all_gather(up_weight, "dep", axis=0, tiled=True),
    )
    qkv_flat = qkv_all.reshape(qkv_all.shape[0], 3 * attn_here)

    def first_term(start, count):
        return jnp.concatenate(
            [
                jnp.dot(group_in, qkv_flat, preferred_element_type=jnp.float32),
                jnp.dot(group_in, up_all, preferred_element_type=jnp.float32),
            ],
            axis=1,
        )

    projected = token_reduce(first_term, own_rows)
    projected_qkv = projected[:, : 3 * attn_here].reshape(own_rows, 3, heads_here, HEAD_DIM)
    before = projected[:, 3 * attn_here :]
    query_hat, query_inverse = normalize(projected_qkv[:, 0])
    key_hat, key_inverse = normalize(projected_qkv[:, 1])
    query_low = (query_hat * head_gain[0]).astype(jnp.bfloat16)
    key_low = (key_hat * head_gain[1]).astype(jnp.bfloat16)
    value_low = projected_qkv[:, 2].astype(jnp.bfloat16)
    all_keys, all_values = (
        lax.all_gather(key_low, "out", axis=0, tiled=True),
        lax.all_gather(value_low, "out", axis=0, tiled=True),
    )
    scores = (
        jnp.einsum("qhe,khe->hqk", query_low, all_keys, preferred_element_type=jnp.float32) * scale
    )
    highest = jnp.max(scores, axis=-1, keepdims=True)
    raised = jnp.exp(scores - highest)
    mass = jnp.sum(raised, axis=-1, keepdims=True)
    weights = raised / mass
    weights_low = weights.astype(jnp.bfloat16)
    attended = jnp.einsum(
        "hqk,khe->qhe", weights_low, all_values, preferred_element_type=jnp.float32
    )
    attended_low = attended.reshape(own_rows, attn_here).astype(jnp.bfloat16)
    activated, slope = gelu_pair(before)
    activated_low = activated.astype(jnp.bfloat16)
    attended_all, activated_all = head_gather(attended_low, activated_low)
    out_all, down_all = (
        lax.all_gather(out_weight, "dep", axis=0, tiled=True),
        lax.all_gather(down_weight, "dep", axis=0, tiled=True),
    )

    def second_term(start, count):
        return jnp.dot(attended_all, out_all, preferred_element_type=jnp.float32) + jnp.dot(
            activated_all, down_all, preferred_element_type=jnp.float32
        )

    mixed = feature_reduce(second_term, local_rows)
    layer_out = (wide + mixed).astype(jnp.bfloat16)[None]
    grad_all = group_gather(upstream[0])

    def back_term(start, count):
        return jnp.concatenate(
            [
                jnp.dot(grad_all, out_all.T, preferred_element_type=jnp.float32),
                jnp.dot(grad_all, down_all.T, preferred_element_type=jnp.float32),
            ],
            axis=1,
        )

    backward = token_reduce(back_term, own_rows)
    attended_grad = (
        backward[:, :attn_here].astype(jnp.bfloat16).reshape(own_rows, heads_here, HEAD_DIM)
    )
    before_grad = (backward[:, attn_here:] * slope).astype(jnp.bfloat16)
    out_part = jnp.dot(attended_all.T, grad_all, preferred_element_type=jnp.float32)
    down_part = jnp.dot(activated_all.T, grad_all, preferred_element_type=jnp.float32)
    out_weight_grad, down_weight_grad = (
        lax.psum_scatter(
            out_part.astype(jnp.bfloat16), "dep", scatter_dimension=0, tiled=True
        ).astype(jnp.float32),
        lax.psum_scatter(
            down_part.astype(jnp.bfloat16), "dep", scatter_dimension=0, tiled=True
        ).astype(jnp.float32),
    )
    slopes = jnp.einsum(
        "qhe,khe->hqk", attended_grad, all_values, preferred_element_type=jnp.float32
    )
    centre = jnp.sum(weights * slopes, axis=-1, keepdims=True)
    score_grad = (weights * (slopes - centre)).astype(jnp.bfloat16)
    query_grad = (
        jnp.einsum("hqk,khe->qhe", score_grad, all_keys, preferred_element_type=jnp.float32) * scale
    )
    key_terms = (
        jnp.einsum("hqk,qhe->khe", score_grad, query_low, preferred_element_type=jnp.float32)
        * scale
    )
    value_terms = jnp.einsum(
        "hqk,qhe->khe", weights_low, attended_grad, preferred_element_type=jnp.float32
    )
    key_grad, value_grad = (
        lax.psum_scatter(key_terms, "out", scatter_dimension=0, tiled=True),
        lax.psum_scatter(value_terms, "out", scatter_dimension=0, tiled=True),
    )
    query_back = normalize_back(query_grad * head_gain[0], query_hat, query_inverse)
    key_back = normalize_back(key_grad * head_gain[1], key_hat, key_inverse)
    gain_part = jnp.stack(
        [jnp.sum(query_grad * query_hat, axis=(0, 1)), jnp.sum(key_grad * key_hat, axis=(0, 1))]
    )
    qkv_grad = (
        jnp.stack([query_back, key_back, value_grad], axis=1)
        .reshape(own_rows, 3, attn_here)
        .astype(jnp.bfloat16)
    )
    qkv_grad_all, before_grad_all = head_gather(qkv_grad, before_grad)
    qkv_part = jnp.einsum("sd,sca->dca", group_in, qkv_grad_all, preferred_element_type=jnp.float32)
    up_part = jnp.dot(group_in.T, before_grad_all, preferred_element_type=jnp.float32)
    qkv_weight_grad, up_weight_grad = (
        lax.psum_scatter(
            qkv_part.astype(jnp.bfloat16), "dep", scatter_dimension=0, tiled=True
        ).astype(jnp.float32),
        lax.psum_scatter(
            up_part.astype(jnp.bfloat16), "dep", scatter_dimension=0, tiled=True
        ).astype(jnp.float32),
    )
    qkv_grad_flat = qkv_grad_all.reshape(group_count, 3 * attn_here)

    def input_term(start, count):
        return jnp.dot(qkv_grad_flat, qkv_flat.T, preferred_element_type=jnp.float32) + jnp.dot(
            before_grad_all, up_all.T, preferred_element_type=jnp.float32
        )

    input_grad = feature_reduce(input_term, local_rows)
    scaled = input_grad * norm_gain
    first_sum, second_sum = row_totals(scaled, scaled * normed)
    centred = scaled - first_sum[:, None] / width - normed * (second_sum[:, None] / width)
    token_grad = (upstream[0].astype(jnp.float32) + inverse[:, None] * centred).astype(
        jnp.bfloat16
    )[None]
    norm_gain_grad = lax.psum(jnp.sum(input_grad * normed, axis=0), ("in", "dep"))
    head_gain_grad = lax.psum(gain_part, ("in", "out", "dep"))
    return (
        layer_out,
        token_grad,
        norm_gain_grad,
        head_gain_grad,
        qkv_weight_grad,
        out_weight_grad,
        up_weight_grad,
        down_weight_grad,
    )


def solution(mesh):
    placed = (
        P("dep", "in", "out"),
        P("out"),
        P(("out", "dep"), None, "in"),
        P(),
        P(("in", "dep"), "out"),
        P(("out", "dep"), "in"),
        P(("in", "dep"), "out"),
        P("dep", "in", "out"),
    )
    return jax.shard_map(
        body,
        mesh=mesh,
        in_specs=placed,
        out_specs=(
            P("dep", "in", "out"),
            P("dep", "in", "out"),
            P("out"),
            P(),
            P(("out", "dep"), None, "in"),
            P(("in", "dep"), "out"),
            P(("out", "dep"), "in"),
            P(("in", "dep"), "out"),
        ),
        check_vma=False,
    )
```

profile of v0, /device:TPU:1, one launch (start us, length us, event | category | flops | bytes accessed | tf_op | source)
XLA Modules:
  0.0 802.9 jit_solution(11225620508008302647)
XLA Ops:
  9.4 29.7 %all_gather.42 = bf16[384,768]{1,0:T(8,128)(2,1)S(1)} all-gather(bf16[48,768]{1,0:T(8,128)(2,1)} %param.12), channel_id=1, replica_groups=mesh['in'=8,'out'=4,'dep'=8] {'dep'}, dimensions={0}, use_global_device_ids=true | all-gather | bytes 663552 | tf_op jit(solution)/shard_map/all_gather | solution.py:121
  39.2 26.3 %all-gather.1 = bf16[1,512,768]{2,1,0:T(8,128)(2,1)S(1)} all-gather(bf16[1,64,768]{2,1,0:T(8,128)(2,1)} %param.15), channel_id=3, replica_groups=mesh['in'=8,'out'=4,'dep'=8] {'in'}, dimensions={1}, use_global_device_ids=true | all-gather | bytes 884736 | tf_op jit(solution)/shard_map/all_gather | solution.py:40
  66.0 10.7 %all-gather.15.cloned.1.call-done = bf16[1536,768]{1,0:T(8,128)(2,1)} async-done(((bf16[192,768]{1,0:T(8,128)(2,1)}), bf16[1536,768]{1,0:T(8,128)(2,1)}) %all-gather.15.cloned.1.call-update) | async-done | bytes 2359312 | tf_op jit(solution)/shard_map/all_gather | solution.py:122
  76.7 3.1 fusion.13
  79.8 2.2 pad_maximum_fusion.1
  83.1 7.9 all-reduce.1
  91.7 25.5 %all_gather.36 = bf16[512,768]{1,0:T(8,128)(2,1)} all-gather(bf16[64,768]{1,0:T(8,128)(2,1)S(1)} %fusion.28), channel_id=1, replica_groups=mesh['in'=8,'out'=4,'dep'=8] {'in'}, dimensions={0}, use_global_device_ids=true | all-gather | bytes 884736 | tf_op jit(solution)/shard_map/all_gather | solution.py:40
  117.2 9.6 %all-gather.9.cloned.1.call-done = bf16[768,3,384]{2,0,1:T(8,128)(2,1)} async-done(((bf16[96,3,384]{2,0,1:T(8,128)(2,1)}), bf16[768,3,384]{2,0,1:T(8,128)(2,1)}) %all-gather.9.cloned.1.call-update) | async-done | bytes 1769488 | tf_op jit(solution)/shard_map/all_gather | solution.py:79
  126.8 2.6 copy.35
  129.4 3.8 fusion.53
  133.2 55.1 %all-gather.11.cloned.1.call-done = bf16[768,1536]{1,0:T(8,128)(2,1)} async-done(((bf16[96,1536]{1,0:T(8,128)(2,1)}), bf16[768,1536]{1,0:T(8,128)(2,1)}) %all-gather.11.cloned.1.call-update) | async-done | bytes 2359312 | tf_op jit(solution)/shard_map/all_gather | solution.py:80
  188.2 3.4 fusion.54
  191.7 2.7 pad_maximum_fusion
  195.1 52.0 %reduce-scatter.15.cloned.1.call-done = f32[128,1920]{1,0:T(8,128)} async-done(((f32[512,1920]{1,0:T(8,128)}), f32[128,1920]{1,0:T(8,128)}) %reduce-scatter.15.cloned.1.call-update) | async-done | bytes 983056 | tf_op jit(solution)/shard_map/reduce_scatter | solution.py:51
  248.8 65.8 %reduce-scatter.11.cloned.1.call-done = f32[128,2688]{1,0:T(8,128)} async-done(((f32[512,2688]{1,0:T(8,128)}), f32[128,2688]{1,0:T(8,128)}) %reduce-scatter.11.cloned.1.call-update) | async-done | bytes 1376272 | tf_op jit(solution)/shard_map/reduce_scatter | solution.py:51
  316.5 8.1 %all_gather.40 = bf16[512,3,128]{2,0,1:T(8,128)(2,1)S(1)} all-gather(bf16[128,3,128]{2,0,1:T(8,128)(2,1)S(1)} %multiply_convert_fusion.3), channel_id=1, replica_groups=mesh['in'=8,'out'=4,'dep'=8] {'out'}, dimensions={0}, use_global_device_ids=true | all-gather | bytes 491520 | tf_op jit(solution)/shard_map/all_gather | solution.py:102
  324.7 8.5 %all-gather = bf16[512,1,3,128]{0,3,2,1:T(8,128)(2,1)} all-gather(bf16[128,1,3,128]{0,3,2,1:T(8,128)(2,1)S(1)} %slice.74), channel_id=2, replica_groups=mesh['in'=8,'out'=4,'dep'=8] {'out'}, dimensions={0}, use_global_device_ids=true | all-gather | bytes 491520 | tf_op jit(solution)/shard_map/all_gather | solution.py:103
  334.9 1.6 multiply_reduce_fusion
  336.6 1.3 multiply_convert_fusion
  339.2 1.5 convolution_bitcast_fusion
  340.7 2.6 fusion.9
  344.1 29.4 %reduce-scatter.17.cloned.1.call-done = f32[128,3,128]{2,0,1:T(8,128)} async-done(((f32[512,3,128]{2,0,1:T(8,128)}), f32[128,3,128]{2,0,1:T(8,128)}) %reduce-scatter.17.cloned.1.call-update) | async-done | bytes 196624 | tf_op jit(solution)/shard_map/reduce_scatter | solution.py:174
  373.5 1.2 multiply_reduce_fusion.1
  374.8 1.2 multiply_convert_fusion.2
  376.2 35.1 %reduce-scatter.19.cloned.1.call-done = f32[128,3,128]{0,2,1:T(8,128)} async-done(((f32[512,3,128]{0,2,1:T(8,128)}), f32[128,3,128]{0,2,1:T(8,128)}) %reduce-scatter.19.cloned.1.call-update) | async-done | bytes 196624 | tf_op jit(solution)/shard_map/reduce_scatter | solution.py:175
  414.5 8.2 %all_gather.41 = bf16[512,384]{0,1:T(8,128)(2,1)S(1)} all-gather(bf16[128,384]{0,1:T(8,128)(2,1)S(1)} %bitcast.178), channel_id=1, replica_groups=mesh['in'=8,'out'=4,'dep'=8] {'out'}, dimensions={0}, use_global_device_ids=true | all-gather | bytes 491520 | tf_op jit(solution)/shard_map/all_gather | solution.py:45
  422.6 1.3 convolution_convert_fusion.3
  424.2 15.7 %all-gather.19.cloned.1.call-done = bf16[512,1536]{1,0:T(8,128)(2,1)} async-done(((bf16[128,1536]{1,0:T(8,128)(2,1)}), bf16[512,1536]{1,0:T(8,128)(2,1)}) %all-gather.19.cloned.1.call-update) | async-done | bytes 1572880 | tf_op jit(solution)/shard_map/all_gather | solution.py:46
  439.8 4.7 fusion.56
  444.5 20.7 %all-gather.17.cloned.1.call-done = bf16[512,3,384]{2,0,1:T(8,128)(2,1)} async-done(((bf16[128,3,384]{2,0,1:T(8,128)(2,1)}), bf16[512,3,384]{2,0,1:T(8,128)(2,1)}) %all-gather.17.cloned.1.call-update) | async-done | bytes 1179664 | tf_op jit(solution)/shard_map/all_gather | solution.py:45
  465.2 4.7 bitcast_add_fusion
  469.9 23.2 %all-gather.13.cloned.1.call-done = bf16[512,1536]{1,0:T(8,128)(2,1)} async-done(((bf16[128,1536]{1,0:T(8,128)(2,1)}), bf16[512,1536]{1,0:T(8,128)(2,1)}) %all-gather.13.cloned.1.call-update) | async-done | bytes 1572880 | tf_op jit(solution)/shard_map/all_gather | solution.py:46
  493.2 3.5 fusion.55
  496.7 1.8 convolution_add_fusion
  498.6 3.7 convolution_convert_fusion.2
  502.4 4.2 convolution_convert_fusion.1
  506.7 1.3 copy-done.20
  508.1 2.8 convolution_convert_fusion
  510.9 19.9 %reduce-scatter.25.cloned.1.call-done = bf16[48,768]{1,0:T(8,128)(2,1)} async-done(((bf16[384,768]{1,0:T(8,128)(2,1)}), bf16[48,768]{1,0:T(8,128)(2,1)}) %reduce-scatter.25.cloned.1.call-update) | async-done | bytes 73744 | tf_op jit(solution)/shard_map/reduce_scatter | solution.py:151
  530.9 1.6 convert_element_type.94
  532.4 78.9 %psum.47 = f32[2,128]{1,0:T(2,128)} all-reduce(f32[2,128]{1,0:T(2,128)S(1)} %pad_maximum_fusion.3), channel_id=1, replica_groups=mesh['in'=8,'out'=4,'dep'=8] {'in','out','dep'}, use_global_device_ids=true, to_apply=%region_29.0 | all-reduce | flops 256 | bytes 2048 | tf_op jit(solution)/shard_map/psum | solution.py:213
  612.4 7.2 all-reduce
  619.6 130.5 %psum.46 = f32[768]{0:T(1024)} all-reduce(f32[768]{0:T(1024)S(1)} %get-tuple-element.14), channel_id=1, replica_groups=mesh['in'=8,'out'=4,'dep'=8] {'in','dep'}, use_global_device_ids=true, to_apply=%region_26.0 | all-reduce | flops 768 | bytes 6144 | tf_op jit(solution)/shard_map/psum | solution.py:212
  750.2 1.8 fusion.49
  752.0 1.7 convert_element_type.92
  753.7 1.8 convert_element_type.96
  755.5 39.1 %reduce-scatter.29.cloned.1.call-done = bf16[192,768]{1,0:T(8,128)(2,1)} async-done(((bf16[1536,768]{1,0:T(8,128)(2,1)}), bf16[192,768]{1,0:T(8,128)(2,1)}) %reduce-scatter.29.cloned.1.call-update) | async-done | bytes 294928 | tf_op jit(solution)/shard_map/reduce_scatter | solution.py:154
  794.6 1.8 convert_element_type.98
  (114 shorter events, 17.5 us)
Async XLA Ops:
  7.2 69.5 %all-gather.15.cloned.1.call-start = ((), (), s32[]{:S(2)}) async-start(), calls=%async_computation.14 | async-start | bytes 2654208 | tf_op jit(solution)/shard_map/all_gather | solution.py:122
  7.9 118.9 %all-gather.9.cloned.1.call-start = ((), (), s32[]{:S(2)}) async-start(), calls=%async_computation.10 | async-start | bytes 1990656 | tf_op jit(solution)/shard_map/all_gather | solution.py:79
  8.7 179.6 %all-gather.11.cloned.1.call-start = ((), (), s32[]{:S(2)}) async-start(), calls=%async_computation.11 | async-start | bytes 2654208 | tf_op jit(solution)/shard_map/all_gather | solution.py:80
  9.4 237.7 %reduce-scatter.15.cloned.1.call-start = ((), (), s32[]{:S(2)}) async-start(), calls=%async_computation.16 | async-start | bytes 4915200 | tf_op jit(solution)/shard_map/reduce_scatter | solution.py:51
  82.0 0.9 copy-start
  82.0 9.6 %copy-start.7 = (f32[768]{0:T(1024)S(1)}, f32[768]{0:T(1024)}, u32[]{:S(2)}) copy-start(f32[768]{0:T(1024)} %param.9) | copy-start | bytes 9220
  82.0 232.6 %reduce-scatter.11.cloned.1.call-start = ((), (), s32[]{:S(2)}) async-start(), calls=%async_computation.12 | async-start | bytes 6881280 | tf_op jit(solution)/shard_map/reduce_scatter | solution.py:51
  91.0 0.6 copy-start.10
  91.0 0.7 copy-start.12
  188.2 3.4 copy-start.1
  194.4 0.7 copy-start.18
  194.4 179.1 %reduce-scatter.17.cloned.1.call-start = ((), (), s32[]{:S(2)}) async-start(), calls=%async_computation.17 | async-start | bytes 983040 | tf_op jit(solution)/shard_map/reduce_scatter | solution.py:174
  195.1 121.3 %copy-start.14 = (f32[128]{0:T(128)}, f32[128]{0:T(128)S(1)}, u32[]{:S(2)}) copy-start(f32[128]{0:T(128)S(1)} %get-tuple-element.33) | copy-start | bytes 1540
  333.2 0.6 copy-start.8
  334.9 1.6 copy-start.3
  334.9 1.7 copy-start.16
  336.6 2.6 copy-start.6
  336.6 2.6 copy-start.17
  339.1 72.2 %reduce-scatter.19.cloned.1.call-start = ((), (), s32[]{:S(2)}) async-start(), calls=%async_computation.18 | async-start | bytes 983040 | tf_op jit(solution)/shard_map/reduce_scatter | solution.py:175
  340.7 2.8 copy-start.19
  340.7 2.8 copy-start.9
  340.7 32.8 %copy-start.15 = (f32[128]{0:T(128)S(1)}, f32[128]{0:T(128)}, u32[]{:S(2)}) copy-start(f32[128]{0:T(128)} %copy-done.14) | copy-start | bytes 1540
  340.7 99.1 %all-gather.19.cloned.1.call-start = ((), (), s32[]{:S(2)}) async-start(), calls=%async_computation.20 | async-start | bytes 1966080 | tf_op jit(solution)/shard_map/all_gather | solution.py:46
  343.4 121.8 %all-gather.17.cloned.1.call-start = ((), (), s32[]{:S(2)}) async-start(), calls=%async_computation.19 | async-start | bytes 1474560 | tf_op jit(solution)/shard_map/all_gather | solution.py:45
  344.0 69.9 %copy-start.5 = (bf16[512,1,3,128]{0,3,2,1:T(8,128)(2,1)S(1)}, bf16[512,1,3,128]{0,3,2,1:T(8,128)(2,1)}, u32[]{:S(2)}) copy-start(bf16[512,1,3,128]{0,3,2,1:T(8,128)(2,1)} %all-gather) | copy-start | bytes 1179652
  413.2 80.0 %all-gather.13.cloned.1.call-start = ((), (), s32[]{:S(2)}) async-start(), calls=%async_computation.13 | async-start | bytes 1966080 | tf_op jit(solution)/shard_map/all_gather | solution.py:46
  413.8 117.1 %reduce-scatter.25.cloned.1.call-start = ((), (), s32[]{:S(2)}) async-start(), calls=%async_computation.23 | async-start | bytes 663552 | tf_op jit(solution)/shard_map/reduce_scatter | solution.py:151
  423.9 187.3 %reduce-scatter.21.cloned.1.call-start = ((), (), s32[]{:S(2)}) async-start(), calls=%async_computation.21 | async-start | bytes 1769472 | tf_op jit(solution)/shard_map/reduce_scatter | solution.py:57
  469.9 280.3 %reduce-scatter.13.cloned.1.call-start = ((), (), s32[]{:S(2)}) async-start(), calls=%async_computation.15 | async-start | bytes 1769472 | tf_op jit(solution)/shard_map/reduce_scatter | solution.py:57
  496.7 1.9 copy-start.2
  498.6 253.4 %reduce-scatter.23.cloned.1.call-start = ((), (), s32[]{:S(2)}) async-start(), calls=%async_computation.22 | async-start | bytes 1990656 | tf_op jit(solution)/shard_map/reduce_scatter | solution.py:191
  502.4 251.3 %reduce-scatter.27.cloned.1.call-start = ((), (), s32[]{:S(2)}) async-start(), calls=%async_computation.24 | async-start | bytes 2654208 | tf_op jit(solution)/shard_map/reduce_scatter | solution.py:194
  506.6 1.4 copy-start.20
  506.7 287.9 %reduce-scatter.29.cloned.1.call-start = ((), (), s32[]{:S(2)}) async-start(), calls=%async_computation.25 | async-start | bytes 2654208 | tf_op jit(solution)/shard_map/reduce_scatter | solution.py:154
  510.9 100.4 %copy-start.11 = (f32[64]{0:T(128)S(1)}, f32[64]{0:T(128)}, u32[]{:S(2)}) copy-start(f32[64]{0:T(128)} %copy-done.10) | copy-start | bytes 772
  510.9 100.4 %copy-start.13 = (f32[64]{0:T(128)S(1)}, f32[64]{0:T(128)}, u32[]{:S(2)}) copy-start(f32[64]{0:T(128)} %copy-done.12) | copy-start | bytes 772
  510.9 239.3 %copy-start.4 = (bf16[1,64,768]{2,1,0:T(8,128)(2,1)S(1)}, bf16[1,64,768]{2,1,0:T(8,128)(2,1)}, u32[]{:S(2)}) copy-start(bf16[1,64,768]{2,1,0:T(8,128)(2,1)} %param.15) | copy-start | bytes 294916
Sparse Core Ops, SparseCore 0:
  9.8 66.8 all-gather.14
  78.5 48.2 all-gather.8
  128.6 59.6 all-gather.10
  190.9 56.1 reduce-scatter.14
  249.9 64.6 reduce-scatter.10
  339.2 34.2 reduce-scatter.16
  376.5 34.7 reduce-scatter.18
  413.7 26.0 all-gather.18
  441.6 23.4 all-gather.16
  467.4 25.6 all-gather.12
  496.3 34.5 reduce-scatter.24
  533.3 40.3 reduce-scatter.20
  576.2 38.6 reduce-scatter.12
  617.3 51.4 reduce-scatter.22
  671.2 61.5 reduce-scatter.26
  735.2 59.3 reduce-scatter.28
where the time goes:
time: 804 us; the launch traced here: 803 us
  waiting for transfers between devices  379 us (47%)
  blocking collectives  331 us (41%)
  matrix products  44 us (5%)
  other arithmetic  23.8 us (3%)
  between operations  14.3 us (2%)
  local copies, waits for them, and re-layouts  10.3 us (1%)
    psum x1, blocking collectives, body(): lax.psum(jnp.sum(input_grad * normed, axis=0), ('in', 'dep'))  131 us
    reduce_scatter x2, waiting for transfers between devices, token_reduce(): lax.psum_scatter(term(jnp.int32(0), rows * lax.axis_size('out')), 'out',...  118 us
    psum x1, blocking collectives, body(): head_gain_grad = lax.psum(gain_part, ('in', 'out', 'dep'))  78.9 us
    all_gather x1, waiting for transfers between devices, body(): lax.all_gather(up_weight, 'dep', axis=0, tiled=True)  55.1 us
    all_gather x2, blocking collectives, group_gather(): return lax.all_gather(values, 'in', axis=0, tiled=True)  51.7 us
    reduce_scatter x1, waiting for transfers between devices, body(): lax.psum_scatter(down_part.astype(jnp.bfloat16), 'dep', scatter_dimension...  39.1 us
    all_gather x2, waiting for transfers between devices, head_gather(): lax.all_gather(second, 'out', axis=0, tiled=True)  38.9 us
    reduce_scatter x1, waiting for transfers between devices, body(): lax.psum_scatter(value_terms, 'out', scatter_dimension=0, tiled=True)  35.1 us
  transfers between devices with their start and end apart: 16, of which 12 were waited for; matrix products, arithmetic and copies ran while one was open for 8% of the time, Pallas kernels for 0%

commit v1 on v0

v1 whole, which is shorter than its diff:
```python
import math

import jax
import jax.numpy as jnp
from jax import lax
from jax.experimental import pallas as pl
from jax.experimental.pallas import tpu as pltpu
from jax.sharding import PartitionSpec as P

MESH = pl.DeviceIdType.MESH
EPSILON = 1e-06
ROOT_HALF = 1.0 / math.sqrt(2.0)
ROOT_TWO_PI = math.sqrt(2.0 * math.pi)
SCALE = 128.0 ** (-0.5)
F32 = jnp.float32
BF16 = jnp.bfloat16
VMEM = pltpu.VMEM

TILES = (384, 384, 512, 512)
COLS = (1152, 384, 1536, 1536)
SHARD = ((96, 1152), (48, 768), (96, 1536), (192, 768))
SPLIT = (48, 32, 48, 96)
RING = (1, 7, 2, 6, 3, 5, 4)


def remote(src, dst, send, recv, device):
    return pltpu.make_async_remote_copy(
        src_ref=src, dst_ref=dst, send_sem=send, recv_sem=recv, device_id=device, device_id_type=MESH
    )


class Place:
    def __init__(self):
        self.i = lax.axis_index("in")
        self.o = lax.axis_index("out")
        self.d = lax.axis_index("dep")
        d = self.d
        x, y = d // 2, d % 2
        right, left, far = (x + 1) % 4, (x + 3) % 4, (x + 2) % 4
        self.me = d
        self.r, self.l, self.f = right * 2 + y, left * 2 + y, far * 2 + y
        self.p = x * 2 + 1 - y
        self.rp, self.lp, self.fp = right * 2 + 1 - y, left * 2 + 1 - y, far * 2 + 1 - y
        self.h, self.c = self.o // 2, self.o % 2
        self.mate = self.h * 2 + 1 - self.c
        self.cross = (1 - self.h) * 2 + self.c
        self.mate_at = {"out": self.mate}
        self.cross_at = {"out": self.cross, "dep": self.p}
        self.diag_at = {"out": (1 - self.h) * 2 + 1 - self.c, "dep": self.p}
        self.diag = (1 - self.h) * 2 + 1 - self.c
        self.table = (
            (self.r, self.l, self.me, self.l, "all"),
            (self.l, self.r, self.me, self.r, "all"),
            (self.p, self.p, self.me, self.p, "all"),
            (self.r, self.l, self.l, self.f, "low"),
            (self.l, self.r, self.r, self.f, "high"),
            (self.r, self.l, self.p, self.lp, "all"),
            (self.l, self.r, self.p, self.rp, "all"),
            (self.p, self.p, self.f, self.fp, "all"),
        )


def rows_of(slot, rows, split, part):
    start = slot * rows
    if part == "all":
        return pl.ds(pl.multiple_of(start, 16), rows)
    if part == "low":
        return pl.ds(pl.multiple_of(start, 16), split)
    return pl.ds(pl.multiple_of(start + split, 16), rows - split)


def greet(place):
    barrier = pltpu.get_barrier_semaphore()
    for k in range(1, 8):
        pl.semaphore_signal(barrier, inc=1, device_id={"in": (place.i + k) % 8}, device_id_type=MESH)
        pl.semaphore_signal(barrier, inc=1, device_id={"dep": (place.d + k) % 8}, device_id_type=MESH)
    for peer in (place.mate_at, place.cross_at, place.diag_at):
        pl.semaphore_signal(barrier, inc=1, device_id=peer, device_id_type=MESH)
    pl.semaphore_wait(barrier, 17)


def dot(a, b):
    return lax.dot_general(a, b, (((1,), (0,)), ((), ())), preferred_element_type=F32)


def dot_nt(a, b):
    return lax.dot_general(a, b, (((1,), (1,)), ((), ())), preferred_element_type=F32)


def dot_tn(a, b):
    return lax.dot_general(a, b, (((0,), (0,)), ((), ())), preferred_element_type=F32)


def normalize(values):
    average = jnp.mean(values, axis=-1, keepdims=True)
    spread = jnp.mean(values * values, axis=-1, keepdims=True) - average * average
    inverse = lax.rsqrt(spread + EPSILON)
    return ((values - average) * inverse, inverse)


def normalize_back(incoming, normed, inverse):
    first = jnp.mean(incoming, axis=-1, keepdims=True)
    second = jnp.mean(incoming * normed, axis=-1, keepdims=True)
    return inverse * (incoming - first - normed * second)


def layer_kernel(
    tokens, gain, head_gain, upstream, wq, wo, wu, wd,
    layer_out, token_grad, gain_grad, head_grad, dq, do, du, dd,
    gq, go, gu, gd, hid, grad, normed, inverse, fq, fo, fu, fd,
    stat_out, stat_in, own0, own1, own2, own3, lo0, lo1, lo2, lo3, in0, in1, in2, in3,
    xs_f, xs_q, xs_o, xs_u, xs_d, xr_f, xr_q, xr_o, xr_u, xr_d,
    kv, att, act, bg, qg, qlow, alow, hats, invs, kvpart, kvin, kvs, kvr,
    tok, ups, hid_t, lo_buf, lo_in, tg_buf, tg_in,
    pq, po, pu, pd, rq, ro, ru, rd, zsend0, zsend1, zin0, zin1, zown0, zown1,
    tot_out, tot_in, vz_out, vz_in, vd_out, vd_in, hz_out, hz_in, hd_out, hd_in, ho_out, ho_in,
    gs, gr, gl, zs, zr, ss, sr, ms, mr, cs, cr, bs, br, ks, kr, ws, wr, vs, vr, es, er,
):
    place = Place()
    shards = (wq, wo, wu, wd)
    gathered = (gq, go, gu, gd)
    own, lo, arrived, final = (own0, own1, own2, own3), (lo0, lo1, lo2, lo3), (in0, in1, in2, in3), (fq, fo, fu, fd)
    partial, returned, result = (pq, po, pu, pd), (rq, ro, ru, rd), (dq, do, du, dd)
    greet(place)
    pending = []

    def start(copy):
        copy.start()
        pending.append(copy)

    def local(src, dst, sem):
        copy = pltpu.make_async_copy(src, dst, sem)
        copy.start()
        return copy

    def slots(a, ref, rows):
        return ref.at[:, rows] if a == 0 else ref.at[rows]

    def gather_copy(a, k, receive=False):
        rows, _ = SHARD[a]
        target, _, mine, theirs, part = place.table[k]
        ref = slots(a, gathered[a], rows_of(theirs if receive else mine, rows, SPLIT[a], part))
        source = ref if receive or k > 2 else shards[a]
        return remote(source, ref, gs.at[a, k], gr.at[a, k], {"dep": target})

    def g_send(a, *kinds):
        for k in kinds:
            start(gather_copy(a, k))

    def g_wait(a, *kinds):
        for k in kinds:
            gather_copy(a, k, True).wait_recv()

    own_copies = [None] * 4

    def stage1(a):
        g_send(a, 0, 1, 2)
        rows, _ = SHARD[a]
        own_copies[a] = local(shards[a], slots(a, gathered[a], rows_of(place.me, rows, 0, "all")), gl.at[a])

    def stage2(a):
        g_wait(a, 0)
        g_send(a, 3)
        g_wait(a, 1)
        g_send(a, 4)
        g_wait(a, 2)
        g_send(a, 5, 6)

    def stage3(a):
        g_wait(a, 3, 4)
        g_send(a, 7)

    def stage4(a):
        g_wait(a, 5, 6, 7)
        own_copies[a].wait()

    def z_slot(ref, index):
        return ref.at[pl.ds(pl.multiple_of(index * 64, 64), 64)]

    def z_ring_copy(which, kind, ref, receive=False):
        turn = kind % 4
        if kind < 4:
            target, slot = (place.i + 1) % 8, (place.i + (7 if receive else 8) - turn) % 8
        else:
            target, slot = (place.i + 7) % 8, (place.i + (1 if receive else 0) + turn) % 8
        first = 32 if kind == 7 else 0
        at = ref.at[pl.ds(pl.multiple_of(slot * 64 + first, 32), 32 if turn == 3 else 64)]
        return remote(at, at, zs.at[which, kind], zr.at[which, kind], {"in": target})

    def z_round(which, ref, turn):
        for way in (0, 4):
            if turn > 0:
                z_ring_copy(which, way + turn - 1, ref, True).wait_recv()
            start(z_ring_copy(which, way + turn, ref))

    def z_done(which, ref):
        for way in (0, 4):
            z_ring_copy(which, way + 3, ref, True).wait_recv()

    def zsum_copy(which, k, send, recv):
        to = (place.i + k) % 8
        return remote(z_slot(send, to), recv.at[k - 1], zs.at[which, k - 1], zr.at[which, k - 1], {"in": to})

    def zsum_send(which, send, recv):
        for k in RING:
            start(zsum_copy(which, k, send, recv))

    def zsum_total(which, send, recv, mine):
        total = mine[...]
        for k in RING:
            zsum_copy(which, k, send, recv).wait_recv()
            total = total + recv[k - 1].astype(F32)
        return total

    def fan_copy(axis, index, size, k, send, recv, sem_s, sem_r):
        if axis == "out":
            peer = (place.mate_at, place.cross_at, place.diag_at)[k - 1]
        else:
            peer = {axis: (index + k) % size}
        return remote(send, recv.at[k - 1], sem_s.at[k - 1], sem_r.at[k - 1], peer)

    def fan_send(axis, index, size, send, recv, sem_s, sem_r):
        for k in range(1, size):
            start(fan_copy(axis, index, size, k, send, recv, sem_s, sem_r))

    def fan_total(axis, index, size, send, recv, sem_s, sem_r):
        total = send[...]
        for k in range(1, size):
            fan_copy(axis, index, size, k, send, recv, sem_s, sem_r).wait_recv()
            total = total + recv[k - 1]
        return total

    def out_rows(ref, index):
        return ref.at[pl.ds(pl.multiple_of(index * 128, 128), 128)]

    def out_copy(which, k, ref, receive=False):
        sent = (place.o, place.o, place.cross)[k]
        got = (place.mate, place.cross, place.diag)[k]
        target = (place.mate_at, place.cross_at, place.mate_at)[k]
        rows = out_rows(ref, got if receive else sent)
        return remote(rows, rows, bs.at[which, k], br.at[which, k], target)

    def out_send(which, ref):
        start(out_copy(which, 1, ref))
        start(out_copy(which, 0, ref))

    def out_relay(which, ref):
        out_copy(which, 1, ref, True).wait_recv()
        start(out_copy(which, 2, ref))

    def out_wait(which, ref):
        out_copy(which, 0, ref, True).wait_recv()
        out_copy(which, 2, ref, True).wait_recv()

    def swap_copy(k, source, landing):
        return remote(source, landing, es.at[k], er.at[k], {"dep": place.p})

    def swap_start(k, source, landing, result):
        @pl.when(place.h == 1)
        def _():
            swap_copy(k, source, landing).start()

        @pl.when(place.h == 0)
        def _():
            result[...] = source[...]

    def swap_end(k, source, landing, result):
        @pl.when(place.h == 1)
        def _():
            swap_copy(k, source, landing).wait()
            if result is not landing:
                result[...] = landing[...]

    swap_start(0, tokens, tok, tok)
    swap_start(1, upstream, ups, ups)
    stage1(0)
    stage1(1)
    swap_end(0, tokens, tok, tok)

    wide = tok[...].astype(F32)
    lane = lax.broadcasted_iota(jnp.int32, (64, 128), 1)
    total = jnp.sum(wide, axis=1, keepdims=True)
    square = jnp.sum(wide * wide, axis=1, keepdims=True)
    stat_out[...] = jnp.where(lane < 64, total, square)
    fan_send("out", place.o, 4, stat_out, stat_in, ss.at[0], sr.at[0])
    swap_end(1, upstream, ups, ups)
    z_slot(grad, place.i)[...] = ups[...]
    stats = fan_total("out", place.o, 4, stat_out, stat_in, ss.at[0], sr.at[0])
    average = stats[:, :1] * (1.0 / 3072.0)
    spread = stats[:, 64:65] * (1.0 / 3072.0) - average * average
    inv = lax.rsqrt(spread + EPSILON)
    norm = (wide - average) * inv
    normed[...] = norm
    inverse[...] = jnp.broadcast_to(inv, (64, 128))
    z_slot(hid, place.i)[...] = (norm * gain[...]).astype(BF16)
    z_round(0, hid, 0)
    z_round(1, grad, 0)
    stage2(0)
    z_round(0, hid, 1)
    stage1(2)
    stage2(1)
    z_round(0, hid, 2)
    stage3(0)
    z_round(1, grad, 1)
    z_round(0, hid, 3)
    stage3(1)
    z_round(1, grad, 2)

    def blocks(ref, core):
        return jnp.concatenate(
            [ref[pl.ds(pl.multiple_of(h * 256 + core * 128, 128), 128), :] for h in range(2)], axis=0
        )

    def product(a, core, out):
        left = blocks(hid if a in (0, 2) else grad, core)

        tile = TILES[a]

        @pl.loop(0, COLS[a] // tile)
        def _(t):
            cols = pl.ds(pl.multiple_of(t * tile, 128), tile)
            if a == 0:
                out[:, cols] = dot(left, gathered[a][t])
            elif a == 2:
                out[:, cols] = dot(left, gathered[a][:, cols])
            else:
                out[:, cols] = dot_nt(left, gathered[a][cols, :])

    def mate_copy(a):
        return remote(lo[a], arrived[a], ms.at[a], mr.at[a], place.mate_at)

    def compute(a):
        product(a, 1 - place.c, lo[a])
        start(mate_copy(a))
        product(a, place.c, own[a])

    far_parts = (
        ((xs_f, xr_f, 0, 0, 768), (xs_q, xr_q, 1, 768, 384)),
        ((xs_o, xr_o, 2, 0, 384),),
        ((xs_u, xr_u, 3, 0, 1536),),
        ((xs_d, xr_d, 4, 0, 1536),),
    )

    def cross_copy(send, recv, k):
        return remote(send, recv, cs.at[k], cr.at[k], place.cross_at)

    there = pl.ds(pl.multiple_of((1 - place.h) * 128, 128), 128)
    here = pl.ds(pl.multiple_of(place.h * 128, 128), 128)

    def reduce_near(a):
        mate_copy(a).wait_recv()
        for send, recv, k, first, count in far_parts[a]:
            cols = pl.ds(first, count)
            send[...] = (own[a][there, cols] + arrived[a][there, cols]).astype(send.dtype)
            start(cross_copy(send, recv, k))
        final[a][...] = own[a][here, :] + arrived[a][here, :]

    def reduce_far(a):
        for send, recv, k, first, count in far_parts[a]:
            cross_copy(send, recv, k).wait_recv()
            final[a][:, first : first + count] += recv[...].astype(F32)

    z_done(0, hid)
    stage4(0)
    compute(0)
    z_round(1, grad, 3)
    stage2(2)
    stage1(3)
    reduce_near(0)
    hid_t[...] = hid[...].T
    z_done(1, grad)
    stage4(1)
    compute(1)
    reduce_near(1)
    stage3(2)

    mine = pl.ds(pl.multiple_of(place.o * 128, 128), 128)
    reduce_far(0)
    for j in range(3):
        cols = slice(j * 128, (j + 1) * 128)
        for part in range(2):
            at = slice(part * 384 + j * 128, part * 384 + (j + 1) * 128)
            hat, hat_inv = normalize(fq[:, at])
            hats[:, at] = hat
            invs[:, at] = jnp.broadcast_to(hat_inv, (128, 128))
            low = (hat * head_gain[part : part + 1, :]).astype(BF16)
            if part == 0:
                qlow[:, cols] = low
            else:
                kv[mine, cols] = low
    kv[mine, 384:768] = fq[:, 768:1152].astype(BF16)
    out_send(0, kv)
    stage2(3)
    reduce_far(1)
    alow[...] = fo[...].astype(BF16)
    out_relay(0, kv)
    stage4(2)
    compute(2)
    reduce_near(2)
    stage3(3)
    out_wait(0, kv)

    query_gain = jnp.zeros((1, 128), F32)
    for j in range(3):
        cols = slice(j * 128, (j + 1) * 128)
        vals = slice(384 + j * 128, 384 + (j + 1) * 128)
        query, incoming = qlow[:, cols], alow[:, cols]
        keys, values = kv[:, cols], kv[:, vals]
        scores = dot_nt(query, keys) * SCALE
        raised = jnp.exp(scores - jnp.max(scores, axis=-1, keepdims=True))
        weights = raised / jnp.sum(raised, axis=-1, keepdims=True)
        weights_low = weights.astype(BF16)
        att[mine, cols] = dot(weights_low, values).astype(BF16)
        slopes = dot_nt(incoming, values)
        centre = jnp.sum(weights * slopes, axis=-1, keepdims=True)
        score_grad = (weights * (slopes - centre)).astype(BF16)
        kvpart[:, cols] = dot_tn(score_grad, query) * SCALE
        kvpart[:, vals] = dot_tn(weights_low, incoming)
        query_grad = dot(score_grad, keys) * SCALE
        hat = hats[:, cols]
        query_gain = query_gain + jnp.sum(query_grad * hat, axis=0, keepdims=True)
        back = normalize_back(query_grad * head_gain[0:1, :], hat, invs[:, cols])
        qg[mine, cols] = back.astype(BF16)
    out_send(1, att)

    def kv_near(h):
        rows = pl.ds(pl.multiple_of(h * 256 + (1 - place.c) * 128, 128), 128)
        return remote(kvpart.at[rows], kvin.at[h], ks.at[h], kr.at[h], place.mate_at)

    kv_far = remote(kvs, kvr, ks.at[2], kr.at[2], place.cross_at)
    for h in range(2):
        start(kv_near(h))

    reduce_far(2)

    def before_tile(t):
        cols = pl.ds(pl.multiple_of(t * 512, 512), 512)
        before = fu[:, cols]
        return cols, before, 0.5 * (1.0 + lax.erf(before * ROOT_HALF))

    @pl.loop(0, 3)
    def _(t):
        cols, before, below = before_tile(t)
        act[mine, cols] = (before * below).astype(BF16)
        fu[:, cols] = below + before * jnp.exp(-0.5 * before * before) / ROOT_TWO_PI

    for h in range(2):
        kv_near(h).wait_recv()
    other = pl.ds(pl.multiple_of(place.cross * 128, 128), 128)
    kvs[...] = (kvpart[other, :] + kvin[1 - place.h]).astype(kvs.dtype)
    start(kv_far)
    out_send(2, act)
    stage4(3)
    compute(3)
    out_relay(1, att)
    reduce_near(3)
    kv_far.wait_recv()
    key_gain = jnp.zeros((1, 128), F32)
    for j in range(3):
        cols = slice(j * 128, (j + 1) * 128)
        keys = slice(384 + j * 128, 384 + (j + 1) * 128)
        vals = slice(768 + j * 128, 768 + (j + 1) * 128)
        key_grad = kvpart[mine, cols] + kvin[place.h, :, cols] + kvr[:, cols].astype(F32)
        hat = hats[:, keys]
        key_gain = key_gain + jnp.sum(key_grad * hat, axis=0, keepdims=True)
        back = normalize_back(key_grad * head_gain[1:2, :], hat, invs[:, keys])
        qg[mine, keys] = back.astype(BF16)
        value_grad = kvpart[mine, keys] + kvin[place.h, :, keys] + kvr[:, keys].astype(F32)
        qg[mine, vals] = value_grad.astype(BF16)
    out_send(4, qg)
    row = lax.broadcasted_iota(jnp.int32, (8, 128), 0)
    hz_out[...] = jnp.where(row == 0, query_gain, jnp.where(row == 1, key_gain, 0.0))
    fan_send("in", place.i, 8, hz_out, hz_in, vs.at[0], vr.at[0])

    def weight_product(a):
        tile = TILES[a]
        if a == 0:

            @pl.loop(0, 3)
            def _(t):
                pq[t] = dot(hid_t[...], qg[:, pl.ds(pl.multiple_of(t * tile, 128), tile)]).astype(BF16)
        elif a == 2:

            @pl.loop(0, 3)
            def _(t):
                cols = pl.ds(pl.multiple_of(t * tile, 128), tile)
                pu[:, cols] = dot(hid_t[...], bg[:, cols]).astype(BF16)
        else:
            left = att if a == 1 else act

            @pl.loop(0, COLS[a] // tile)
            def _(t):
                cols = pl.ds(pl.multiple_of(t * tile, 128), tile)
                partial[a][cols, :] = dot_tn(left[:, cols], grad[...]).astype(BF16)

    def back_place(a, k):
        rows, _ = SHARD[a]
        part = place.table[k][4]
        slot = (0, 1, 2, 3, 3, 4, 5, 6)[k]
        if part == "all":
            return returned[a].at[slot]
        if part == "low":
            return slots(a, returned[a].at[slot], pl.ds(0, SPLIT[a]))
        return slots(a, returned[a].at[slot], pl.ds(SPLIT[a], rows - SPLIT[a]))

    def back_copy(a, k):
        rows, _ = SHARD[a]
        _, target, _, slot, part = place.table[k]
        source = slots(a, partial[a], rows_of(slot, rows, SPLIT[a], part))
        return remote(source, back_place(a, k), ws.at[a, k], wr.at[a, k], {"dep": target})

    def b_send(a, *kinds):
        for k in kinds:
            start(back_copy(a, k))

    def b_add(a, *kinds):
        rows, _ = SHARD[a]
        for k in kinds:
            back_copy(a, k).wait_recv()
        _, _, slot, _, part = place.table[kinds[0]]
        at = slots(a, partial[a], rows_of(slot, rows, SPLIT[a], part))
        total = at[...].astype(F32)
        for k in kinds:
            total = total + back_place(a, k)[...].astype(F32)
        return at, total

    def b_merge(a, *kinds):
        at, total = b_add(a, *kinds)
        at[...] = total.astype(BF16)

    def back1(a):
        b_send(a, 7, 5, 6)

    def back2(a):
        b_merge(a, 7)
        b_send(a, 3, 4)
        b_merge(a, 5, 6)
        b_send(a, 2)

    def back3(a):
        b_merge(a, 3)
        b_send(a, 0)
        b_merge(a, 4)
        b_send(a, 1)

    def back4(a):
        _, total = b_add(a, 0, 1, 2)
        result[a][...] = total

    def to_in(which, send, recv, mine_ref, term):
        for b in range(2):
            rows = slice(b * 256, (b + 1) * 256)
            own0[:, :768] = term(rows)
            send[rows, :] = own0[:, :768].astype(BF16)

            @pl.when(place.i // 4 == b)
            def _():
                mine_ref[...] = own0[pl.ds(pl.multiple_of((place.i % 4) * 64, 64), 64), :768]

        zsum_send(which, send, recv)

    out_relay(2, act)
    out_wait(1, att)
    weight_product(1)
    back1(1)
    out_wait(2, act)
    weight_product(3)
    back1(3)
    out_relay(4, qg)
    reduce_far(3)

    @pl.loop(0, 3)
    def _(t):
        cols = pl.ds(pl.multiple_of(t * 512, 512), 512)
        bg[mine, cols] = (fd[:, cols] * fu[:, cols]).astype(BF16)

    out_send(3, bg)
    back2(1)
    to_in(2, zsend0, zin0, zown0, lambda r: dot(att[r, :], go[...]) + dot(act[r, :], gd[...]))
    out_wait(4, qg)
    weight_product(0)
    back1(0)
    back2(3)
    out_relay(3, bg)
    back3(1)
    out_wait(3, bg)
    weight_product(2)
    back1(2)
    back2(0)
    back3(3)

    def input_term(r):
        total = dot_nt(bg[r, :], gu[...])
        for part in range(3):
            total = total + dot_nt(qg[r, part * 384 : (part + 1) * 384], gq[part])
        return total

    to_in(3, zsend1, zin1, zown1, input_term)
    back2(2)
    back3(0)
    hd_out[...] = fan_total("in", place.i, 8, hz_out, hz_in, vs.at[0], vr.at[0])
    fan_send("dep", place.d, 8, hd_out, hd_in, vs.at[1], vr.at[1])
    lo_buf[...] = (tok[...].astype(F32) + zsum_total(2, zsend0, zin0, zown0)).astype(BF16)
    swap_start(2, lo_buf, lo_in, layer_out)

    input_grad = zsum_total(3, zsend1, zin1, zown1)
    scaled = input_grad * gain[...]
    first = jnp.sum(scaled, axis=1, keepdims=True)
    second = jnp.sum(scaled * normed[...], axis=1, keepdims=True)
    tot_out[...] = jnp.where(lane < 64, first, second)
    fan_send("out", place.o, 4, tot_out, tot_in, ss.at[1], sr.at[1])
    vz_out[...] = jnp.sum(input_grad * normed[...], axis=0, keepdims=True)
    fan_send("in", place.i, 8, vz_out, vz_in, vs.at[2], vr.at[2])
    back3(2)
    totals = fan_total("out", place.o, 4, tot_out, tot_in, ss.at[1], sr.at[1])
    centred = scaled - totals[:, :1] * (1.0 / 3072.0) - normed[...] * (totals[:, 64:65] * (1.0 / 3072.0))
    tg_buf[...] = (ups[...].astype(F32) + inverse[:, :1] * centred).astype(BF16)
    swap_start(3, tg_buf, tg_in, token_grad)
    vd_out[...] = fan_total("in", place.i, 8, vz_out, vz_in, vs.at[2], vr.at[2])
    fan_send("dep", place.d, 8, vd_out, vd_in, vs.at[3], vr.at[3])
    ho_out[...] = fan_total("dep", place.d, 8, hd_out, hd_in, vs.at[1], vr.at[1])
    fan_send("out", place.o, 4, ho_out, ho_in, ss.at[2], sr.at[2])
    back4(1)
    back4(3)
    back4(2)
    back4(0)
    head_grad[...] = fan_total("out", place.o, 4, ho_out, ho_in, ss.at[2], sr.at[2])[:2]
    swap_end(2, lo_buf, lo_in, layer_out)
    swap_end(3, tg_buf, tg_in, token_grad)
    gain_grad[...] = fan_total("dep", place.d, 8, vd_out, vd_in, vs.at[3], vr.at[3])
    for copy in pending:
        copy.wait_send()


def layer(tokens, gain, head_gain, upstream, wq, wo, wu, wd):
    shape = jax.ShapeDtypeStruct
    outs = [
        shape((64, 768), BF16), shape((64, 768), BF16), shape((1, 768), F32), shape((2, 128), F32),
        shape((3, 96, 384), F32), shape((48, 768), F32), shape((96, 1536), F32), shape((192, 768), F32),
    ]
    whole = pl.BlockSpec(memory_space=VMEM)
    far = [VMEM((128, 768), F32), VMEM((128, 384), BF16), VMEM((128, 384), BF16), VMEM((128, 1536), BF16), VMEM((128, 1536), BF16)]
    full = [VMEM((3, 768, 384), BF16), VMEM((384, 768), BF16), VMEM((768, 1536), BF16), VMEM((1536, 768), BF16)]
    scratch = full + [VMEM((512, 768), BF16), VMEM((512, 768), BF16), VMEM((64, 768), F32), VMEM((64, 128), F32)]
    scratch += [VMEM((128, n), F32) for n in COLS]
    scratch += [VMEM((64, 128), F32), VMEM((3, 64, 128), F32)]
    for _ in range(3):
        scratch += [VMEM((256, n), F32) for n in COLS]
    scratch += far + far
    scratch += [VMEM((512, n), BF16) for n in (768, 384, 1536, 1536, 1152)]
    scratch += [VMEM((128, 384), BF16), VMEM((128, 384), BF16), VMEM((128, 768), F32), VMEM((128, 768), F32)]
    scratch += [VMEM((512, 768), F32), VMEM((2, 128, 768), F32), VMEM((128, 768), BF16), VMEM((128, 768), BF16)]
    scratch += [VMEM((64, 768), BF16)] * 2 + [VMEM((768, 512), BF16)] + [VMEM((64, 768), BF16)] * 4
    scratch += full + [VMEM((7, 3, 96, 384), BF16)] + [VMEM((7, rows, cols), BF16) for rows, cols in SHARD[1:]]
    scratch += [VMEM((512, 768), BF16)] * 2 + [VMEM((7, 64, 768), BF16)] * 2 + [VMEM((64, 768), F32)] * 2
    scratch += [VMEM((64, 128), F32), VMEM((3, 64, 128), F32)]
    scratch += [VMEM((1, 768), F32), VMEM((7, 1, 768), F32)] * 2
    scratch += [VMEM((8, 128), F32), VMEM((7, 8, 128), F32)] * 2
    scratch += [VMEM((8, 128), F32), VMEM((3, 8, 128), F32)]
    dma = pltpu.SemaphoreType.DMA
    scratch += [dma((4, 8)), dma((4, 8)), dma((4,)), dma((4, 8)), dma((4, 8)), dma((3, 3)), dma((3, 3))]
    scratch += [dma((4,)), dma((4,)), dma((5,)), dma((5,)), dma((5, 3)), dma((5, 3)), dma((3,)), dma((3,))]
    scratch += [dma((4, 8)), dma((4, 8)), dma((4, 7)), dma((4, 7)), dma((4,)), dma((4,))]
    return pl.pallas_call(
        layer_kernel,
        out_shape=outs,
        in_specs=[whole] * 4 + [pl.BlockSpec(memory_space=pl.ANY)] * 4,
        out_specs=[whole] * len(outs),
        scratch_shapes=scratch,
        compiler_params=pltpu.CompilerParams(collective_id=1, has_side_effects=True, vmem_limit_bytes=62 * 2**20),
        cost_estimate=pl.CostEstimate(flops=11 * 10**9, bytes_accessed=10**7, transcendentals=10**6),
    )(tokens, gain, head_gain, upstream, wq, wo, wu, wd)


def body(tokens, norm_gain, qkv_weight, head_gain, out_weight, up_weight, down_weight, upstream):
    layer_out, token_grad, gain_grad, head_grad, dq, do, du, dd = layer(
        tokens[0], norm_gain[None], head_gain, upstream[0],
        jnp.transpose(qkv_weight, (1, 0, 2)), out_weight, up_weight, down_weight,
    )
    return (
        layer_out[None], token_grad[None], gain_grad[0], head_grad,
        jnp.transpose(dq, (1, 0, 2)), do, du, dd,
    )


def solution(mesh):
    placed = (
        P("dep", "in", "out"),
        P("out"),
        P(("out", "dep"), None, "in"),
        P(),
        P(("in", "dep"), "out"),
        P(("out", "dep"), "in"),
        P(("in", "dep"), "out"),
        P("dep", "in", "out"),
    )
    return jax.shard_map(
        body,
        mesh=mesh,
        in_specs=placed,
        out_specs=(
            P("dep", "in", "out"),
            P("dep", "in", "out"),
            P("out"),
            P(),
            P(("out", "dep"), None, "in"),
            P(("in", "dep"), "out"),
            P(("out", "dep"), "in"),
            P(("in", "dep"), "out"),
        ),
        check_vma=False,
    )
```

time: 804 us -> 172 us (0.21)
  waiting for transfers between devices: 379 us -> 0 us
  blocking collectives: 331 us -> 0 us
  Pallas kernels: 0 us -> 161 us
  matrix products: 44 us -> 0 us
  other arithmetic: 23.8 us -> 0.6 us
  between operations: 14.3 us -> 0.66 us
    reduce_scatter x10 -> x0, waiting for transfers between devices: 241 us -> none  [the longest x2 118 us: token_reduce(): lax.psum_scatter(term(jnp.int32(0), rows * lax.axis_size('out')), 'out',...]
    psum x4 -> x0, blocking collectives: 224 us -> none  [the longest x1 131 us: body(): lax.psum(jnp.sum(input_grad * normed, axis=0), ('in', 'dep'))]
    pallas_call x0 -> x1, Pallas kernels: none -> 161 us  [layer(): pl.pallas_call(layer_kernel, out_shape=outs, in_specs=[whole] * 4 + [pl.B...]
    all_gather x6 -> x0, waiting for transfers between devices: 135 us -> none  [the longest x1 55.1 us: body(): lax.all_gather(up_weight, 'dep', axis=0, tiled=True)]
    all_gather x6 -> x0, blocking collectives: 106 us -> none  [the longest x2 51.7 us: group_gather(): return lax.all_gather(values, 'in', axis=0, tiled=True)]
    dot_general x17 -> x0, matrix products: 42.9 us -> none  [the longest x1 4.7 us: input_term(): jnp.dot(before_grad_all, up_all.T, preferred_element_type=jnp.float32)]
    convert_element_type x9 -> x0, other arithmetic: 11.2 us -> none  [the longest x2 3.56 us: body(): qkv_weight_grad, up_weight_grad = (lax.psum_scatter(qkv_part.astype(jnp.b...]
  transfers between devices with their start and end apart: 16 -> 0, of which waited for: 12 -> 0; matrix products, arithmetic and copies ran while one was open for 8% -> 0% of each run, Pallas kernels for 0% -> 0%
where the time goes in v1:
time: 172 us
  Pallas kernels  161 us (94%)
  local copies, waits for them, and re-layouts  9.38 us (5%)
    pallas_call x1, Pallas kernels, layer(): pl.pallas_call(layer_kernel, out_shape=outs, in_specs=[whole] * 4 + [pl.B...  161 us
    unnamed x19, local copies, waits for them, and re-layouts  8.11 us

profile of v1, /device:TPU:1, one launch (start us, length us, event | category | flops | bytes accessed | tf_op | source)
XLA Modules:
  0.0 171.8 jit_solution(2174685015690054136)
XLA Ops:
  0.6 1.3 broadcast_in_dim.9.gain
  1.9 161.1 %shard_map.143 = (bf16[64,768]{1,0:T(8,128)(2,1)}, bf16[64,768]{1,0:T(8,128)(2,1)}, f32[1,768]{1,0:T(1,128)}, f32[2,128]{1,0:T(2,128)}, f32[3,96,384]{2,1,0:T(8,...) custom-call(bf16[64,768]{1,0:T(8,128)(2,1)} %bitcast.10, f32[1,768]{1,0:T(1,128)} %broadcast_in_dim.9.gain, ...), custom_call_target="tpu_custom_call" | custom-call | flops 11000000512 | bytes 10000000 | tf_op jit(solution)/shard_map/pallas_call | solution.py:664
  163.0 0.0 copy-start.4
  163.1 0.7 copy-done.4
  163.7 0.6 reduce
  164.3 0.0 copy-start.3
  164.3 1.6 copy.23
  165.9 0.0 copy-done.3
  165.9 0.0 copy-start.5
  165.9 0.6 copy.24
  166.6 0.0 copy-done.5
  166.6 0.6 copy.25
  167.1 0.0 copy-start.2
  167.2 0.0 copy-start.1
  167.2 1.9 %copy.26 = f32[96,3,384]{2,0,1:T(8,128)} copy(f32[96,3,384]{2,0,1:T(8,128)} %bitcast.6) | data formatting | bytes 884736
  169.0 0.0 copy-done.2
  169.0 0.7 copy.27
  169.7 0.0 copy-done.1
  169.7 0.0 copy-start
  169.7 0.8 copy.28
  170.5 0.5 copy-done
  171.0 0.8 copy.29
Async XLA Ops:
  163.0 0.7 copy-start.4
  164.3 1.6 copy-start.3
  165.9 0.7 copy-start.5
  167.1 1.9 %copy-start.2 = (f32[48,768]{1,0:T(8,128)S(1)}, f32[48,768]{1,0:T(8,128)}, u32[]{:S(2)}) copy-start(f32[48,768]{1,0:T(8,128)} %get-tuple-element.37) | copy-start | bytes 442372
  167.2 2.5 %copy-start.1 = (f32[96,1536]{1,0:T(8,128)S(1)}, f32[96,1536]{1,0:T(8,128)}, u32[]{:S(2)}) copy-start(f32[96,1536]{1,0:T(8,128)} %get-tuple-element.38) | copy-start | bytes 1769476
  169.7 1.3 copy-start

commit v2 on v1

--- a/solution.py
+++ b/solution.py
@@ -108,18 +108,18 @@
     tokens, gain, head_gain, upstream, wq, wo, wu, wd,
     layer_out, token_grad, gain_grad, head_grad, dq, do, du, dd,
     gq, go, gu, gd, hid, grad, normed, inverse, fq, fo, fu, fd,
-    stat_out, stat_in, own0, own1, own2, own3, lo0, lo1, lo2, lo3, in0, in1, in2, in3,
+    stat_out, stat_in, away0, away1, away2, away3, home0, home1, home2, home3, in0, in1, in2, in3,
     xs_f, xs_q, xs_o, xs_u, xs_d, xr_f, xr_q, xr_o, xr_u, xr_d,
     kv, att, act, bg, qg, qlow, alow, hats, invs, kvpart, kvin, kvs, kvr,
     tok, ups, hid_t, lo_buf, lo_in, tg_buf, tg_in,
-    pq, po, pu, pd, rq, ro, ru, rd, zsend0, zsend1, zin0, zin1, zown0, zown1,
+    pq, po, pu, pd, rq, ro, ru, rd, zsend0, zin0, zown0, ring_out, ring_in,
     tot_out, tot_in, vz_out, vz_in, vd_out, vd_in, hz_out, hz_in, hd_out, hd_in, ho_out, ho_in,
     gs, gr, gl, zs, zr, ss, sr, ms, mr, cs, cr, bs, br, ks, kr, ws, wr, vs, vr, es, er,
 ):
     place = Place()
     shards = (wq, wo, wu, wd)
     gathered = (gq, go, gu, gd)
-    own, lo, arrived, final = (own0, own1, own2, own3), (lo0, lo1, lo2, lo3), (in0, in1, in2, in3), (fq, fo, fu, fd)
+    away, home, arrived, final = (away0, away1, away2, away3), (home0, home1, home2, home3), (in0, in1, in2, in3), (fq, fo, fu, fd)
     partial, returned, result = (pq, po, pu, pd), (rq, ro, ru, rd), (dq, do, du, dd)
     greet(place)
     pending = []
@@ -297,23 +297,16 @@
     z_round(1, grad, 0)
     stage2(0)
     z_round(0, hid, 1)
+    stage2(1)
     stage1(2)
-    stage2(1)
     z_round(0, hid, 2)
     stage3(0)
+    z_round(0, hid, 3)
     z_round(1, grad, 1)
-    z_round(0, hid, 3)
     stage3(1)
-    z_round(1, grad, 2)
-
-    def blocks(ref, core):
-        return jnp.concatenate(
-            [ref[pl.ds(pl.multiple_of(h * 256 + core * 128, 128), 128), :] for h in range(2)], axis=0
-        )
-
-    def product(a, core, out):
-        left = blocks(hid if a in (0, 2) else grad, core)
-
+
+    def product(a, half, out):
+        left = (hid if a in (0, 2) else grad)[pl.ds(pl.multiple_of(half * 256, 256), 256), :]
         tile = TILES[a]
 
         @pl.loop(0, COLS[a] // tile)
@@ -326,13 +319,13 @@
             else:
                 out[:, cols] = dot_nt(left, gathered[a][cols, :])
 
-    def mate_copy(a):
-        return remote(lo[a], arrived[a], ms.at[a], mr.at[a], place.mate_at)
-
-    def compute(a):
-        product(a, 1 - place.c, lo[a])
-        start(mate_copy(a))
-        product(a, place.c, own[a])
+    theirs = pl.ds(pl.multiple_of((1 - place.c) * 128, 128), 128)
+    ours = pl.ds(pl.multiple_of(place.c * 128, 128), 128)
+
+    def mate_copy(a, k):
+        return remote(
+            (away, home)[k][a].at[theirs], arrived[a].at[pl.ds(k * 128, 128)], ms.at[a, k], mr.at[a, k], place.mate_at
+        )
 
     far_parts = (
         ((xs_f, xr_f, 0, 0, 768), (xs_q, xr_q, 1, 768, 384)),
@@ -344,35 +337,38 @@
     def cross_copy(send, recv, k):
         return remote(send, recv, cs.at[k], cr.at[k], place.cross_at)
 
-    there = pl.ds(pl.multiple_of((1 - place.h) * 128, 128), 128)
-    here = pl.ds(pl.multiple_of(place.h * 128, 128), 128)
-
-    def reduce_near(a):
-        mate_copy(a).wait_recv()
+    def compute(a):
+        product(a, 1 - place.h, away[a])
+        mate_copy(a, 0).start()
+        product(a, place.h, home[a])
+        mate_copy(a, 1).start()
+        mate_copy(a, 0).wait_recv()
         for send, recv, k, first, count in far_parts[a]:
-            cols = pl.ds(first, count)
-            send[...] = (own[a][there, cols] + arrived[a][there, cols]).astype(send.dtype)
+            cols = slice(first, first + count)
+            send[...] = (away[a][ours, cols] + arrived[a][:128, cols]).astype(send.dtype)
             start(cross_copy(send, recv, k))
-        final[a][...] = own[a][here, :] + arrived[a][here, :]
 
     def reduce_far(a):
+        mate_copy(a, 1).wait_recv()
         for send, recv, k, first, count in far_parts[a]:
+            cols = slice(first, first + count)
             cross_copy(send, recv, k).wait_recv()
-            final[a][:, first : first + count] += recv[...].astype(F32)
+            final[a][:, cols] = home[a][ours, cols] + arrived[a][128:, cols] + recv[...].astype(F32)
+        for k in range(2):
+            mate_copy(a, k).wait_send()
 
     z_done(0, hid)
     stage4(0)
     compute(0)
-    z_round(1, grad, 3)
+    z_round(1, grad, 2)
     stage2(2)
     stage1(3)
-    reduce_near(0)
-    hid_t[...] = hid[...].T
+    z_round(1, grad, 3)
+    stage3(2)
     z_done(1, grad)
     stage4(1)
     compute(1)
-    reduce_near(1)
-    stage3(2)
+    hid_t[...] = hid[...].T
 
     mine = pl.ds(pl.multiple_of(place.o * 128, 128), 128)
     reduce_far(0)
@@ -390,18 +386,15 @@
                 kv[mine, cols] = low
     kv[mine, 384:768] = fq[:, 768:1152].astype(BF16)
     out_send(0, kv)
-    stage2(3)
+    stage4(2)
+    compute(2)
+    out_relay(0, kv)
     reduce_far(1)
     alow[...] = fo[...].astype(BF16)
-    out_relay(0, kv)
-    stage4(2)
-    compute(2)
-    reduce_near(2)
-    stage3(3)
+    stage2(3)
     out_wait(0, kv)
 
-    query_gain = jnp.zeros((1, 128), F32)
-    for j in range(3):
+    def attend(j):
         cols = slice(j * 128, (j + 1) * 128)
         vals = slice(384 + j * 128, 384 + (j + 1) * 128)
         query, incoming = qlow[:, cols], alow[:, cols]
@@ -418,25 +411,26 @@
         kvpart[:, vals] = dot_tn(weights_low, incoming)
         query_grad = dot(score_grad, keys) * SCALE
         hat = hats[:, cols]
-        query_gain = query_gain + jnp.sum(query_grad * hat, axis=0, keepdims=True)
+        gain_part = jnp.sum(query_grad * hat, axis=0, keepdims=True)
         back = normalize_back(query_grad * head_gain[0:1, :], hat, invs[:, cols])
         qg[mine, cols] = back.astype(BF16)
-    out_send(1, att)
+        return gain_part
 
     def kv_near(h):
         rows = pl.ds(pl.multiple_of(h * 256 + (1 - place.c) * 128, 128), 128)
         return remote(kvpart.at[rows], kvin.at[h], ks.at[h], kr.at[h], place.mate_at)
 
     kv_far = remote(kvs, kvr, ks.at[2], kr.at[2], place.cross_at)
-    for h in range(2):
-        start(kv_near(h))
-
-    reduce_far(2)
-
     def before_tile(t):
         cols = pl.ds(pl.multiple_of(t * 512, 512), 512)
         before = fu[:, cols]
         return cols, before, 0.5 * (1.0 + lax.erf(before * ROOT_HALF))
+
+    query_gain = attend(0)
+    stage3(3)
+    query_gain = query_gain + attend(1)
+
+    reduce_far(2)
 
     @pl.loop(0, 3)
     def _(t):
@@ -444,16 +438,143 @@
         act[mine, cols] = (before * below).astype(BF16)
         fu[:, cols] = below + before * jnp.exp(-0.5 * before * before) / ROOT_TWO_PI
 
+    out_send(2, act)
+    query_gain = query_gain + attend(2)
+    for h in range(2):
+        start(kv_near(h))
+    out_send(1, att)
     for h in range(2):
         kv_near(h).wait_recv()
     other = pl.ds(pl.multiple_of(place.cross * 128, 128), 128)
     kvs[...] = (kvpart[other, :] + kvin[1 - place.h]).astype(kvs.dtype)
     start(kv_far)
-    out_send(2, act)
     stage4(3)
     compute(3)
+    def weight_product(a):
+        tile = TILES[a]
+        if a == 0:
+
+            @pl.loop(0, 3)
+            def _(t):
+                pq[t] = dot(hid_t[...], qg[:, pl.ds(pl.multiple_of(t * tile, 128), tile)]).astype(BF16)
+        elif a == 2:
+
+            @pl.loop(0, 3)
+            def _(t):
+                cols = pl.ds(pl.multiple_of(t * tile, 128), tile)
+                pu[:, cols] = dot(hid_t[...], bg[:, cols]).astype(BF16)
+        else:
+            left = att if a == 1 else act
+
+            @pl.loop(0, COLS[a] // tile)
+            def _(t):
+                cols = pl.ds(pl.multiple_of(t * tile, 128), tile)
+                partial[a][cols, :] = dot_tn(left[:, cols], grad[...]).astype(BF16)
+
+    def back_place(a, k):
+        rows, _ = SHARD[a]
+        part = place.table[k][4]
+        slot = (0, 1, 2, 3, 3, 4, 5, 6)[k]
+        if part == "all":
+            return returned[a].at[slot]
+        if part == "low":
+            return slots(a, returned[a].at[slot], pl.ds(0, SPLIT[a]))
+        return slots(a, returned[a].at[slot], pl.ds(SPLIT[a], rows - SPLIT[a]))
+
+    def back_copy(a, k):
+        rows, _ = SHARD[a]
+        _, target, _, slot, part = place.table[k]
+        source = slots(a, partial[a], rows_of(slot, rows, SPLIT[a], part))
+        return remote(source, back_place(a, k), ws.at[a, k], wr.at[a, k], {"dep": target})
+
+    def b_send(a, *kinds):
+        for k in kinds:
+            start(back_copy(a, k))
+
+    def b_add(a, *kinds):
+        rows, _ = SHARD[a]
+        for k in kinds:
+            back_copy(a, k).wait_recv()
+        _, _, slot, _, part = place.table[kinds[0]]
+        at = slots(a, partial[a], rows_of(slot, rows, SPLIT[a], part))
+        total = at[...].astype(F32)
+        for k in kinds:
+            total = total + back_place(a, k)[...].astype(F32)
+        return at, total
+
+    def b_merge(a, *kinds):
+        at, total = b_add(a, *kinds)
+        at[...] = total.astype(BF16)
+
+    def back1(a):
+        b_send(a, 7, 5, 6)
+
+    def back2(a):
+        b_merge(a, 7)
+        b_send(a, 3, 4)
+        b_merge(a, 5, 6)
+        b_send(a, 2)
+
+    def back3(a):
+        b_merge(a, 3)
+        b_send(a, 0)
+        b_merge(a, 4)
+        b_send(a, 1)
+
+    def back4(a):
+        _, total = b_add(a, 0, 1, 2)
+        result[a][...] = total
+
+    def to_in(which, send, recv, mine_ref, term):
+        for b in range(2):
+            rows = slice(b * 256, (b + 1) * 256)
+            home0[:, :768] = term(rows)
+            send[rows, :] = home0[:, :768].astype(BF16)
+
+            @pl.when(place.i // 4 == b)
+            def _():
+                mine_ref[...] = home0[pl.ds(pl.multiple_of((place.i % 4) * 64, 64), 64), :768]
+
+        zsum_send(which, send, recv)
+
+    def block_of(index):
+        index = index % 8
+        rows = pl.ds(pl.multiple_of((index % 4) * 64, 64), 64)
+        return away2.at[rows, pl.ds(pl.multiple_of((index // 4) * 768, 128), 768)]
+
+    def ring_copy(way, step):
+        target = (place.i + (1, 7)[way]) % 8
+        rows = (pl.ds(0, 32), pl.ds(32, 32))[way] if step == 0 else pl.ds(0, 64)
+        at = (way, step, rows)
+        return remote(ring_out.at[at], ring_in.at[at], zs.at[3, way * 4 + step], zr.at[3, way * 4 + step], {"in": target})
+
+    def ring_step(step):
+        for way in range(2):
+            block = block_of(place.i + (4 - step, 4 + step)[way])
+            if step == 0:
+                ring_out[way, 0] = block[...].astype(BF16)
+            else:
+                ring_copy(way, step - 1).wait_recv()
+                if step == 1:
+                    half = (slice(0, 32), slice(32, 64))[way]
+                    block[half, :] += ring_in[way, 0, half, :].astype(F32)
+                    ring_out[way, 1] = block[...].astype(BF16)
+                else:
+                    ring_out[way, step] = (block[...] + ring_in[way, step - 1].astype(F32)).astype(BF16)
+            start(ring_copy(way, step))
+
+    def ring_total():
+        total = block_of(place.i)[...]
+        for way in range(2):
+            ring_copy(way, 3).wait_recv()
+            total = total + ring_in[way, 3].astype(F32)
+        return total
+
+    out_relay(2, act)
+    out_wait(2, act)
+    weight_product(3)
+    back1(3)
     out_relay(1, att)
-    reduce_near(3)
     kv_far.wait_recv()
     key_gain = jnp.zeros((1, 128), F32)
     for j in range(3):
@@ -472,101 +593,11 @@
     hz_out[...] = jnp.where(row == 0, query_gain, jnp.where(row == 1, key_gain, 0.0))
     fan_send("in", place.i, 8, hz_out, hz_in, vs.at[0], vr.at[0])
 
-    def weight_product(a):
-        tile = TILES[a]
-        if a == 0:
-
-            @pl.loop(0, 3)
-            def _(t):
-                pq[t] = dot(hid_t[...], qg[:, pl.ds(pl.multiple_of(t * tile, 128), tile)]).astype(BF16)
-        elif a == 2:
-
-            @pl.loop(0, 3)
-            def _(t):
-                cols = pl.ds(pl.multiple_of(t * tile, 128), tile)
-                pu[:, cols] = dot(hid_t[...], bg[:, cols]).astype(BF16)
-        else:
-            left = att if a == 1 else act
-
-            @pl.loop(0, COLS[a] // tile)
-            def _(t):
-                cols = pl.ds(pl.multiple_of(t * tile, 128), tile)
-                partial[a][cols, :] = dot_tn(left[:, cols], grad[...]).astype(BF16)
-
-    def back_place(a, k):
-        rows, _ = SHARD[a]
-        part = place.table[k][4]
-        slot = (0, 1, 2, 3, 3, 4, 5, 6)[k]
-        if part == "all":
-            return returned[a].at[slot]
-        if part == "low":
-            return slots(a, returned[a].at[slot], pl.ds(0, SPLIT[a]))
-        return slots(a, returned[a].at[slot], pl.ds(SPLIT[a], rows - SPLIT[a]))
-
-    def back_copy(a, k):
-        rows, _ = SHARD[a]
-        _, target, _, slot, part = place.table[k]
-        source = slots(a, partial[a], rows_of(slot, rows, SPLIT[a], part))
-        return remote(source, back_place(a, k), ws.at[a, k], wr.at[a, k], {"dep": target})
-
-    def b_send(a, *kinds):
-        for k in kinds:
-            start(back_copy(a, k))
-
-    def b_add(a, *kinds):
-        rows, _ = SHARD[a]
-        for k in kinds:
-            back_copy(a, k).wait_recv()
-        _, _, slot, _, part = place.table[kinds[0]]
-        at = slots(a, partial[a], rows_of(slot, rows, SPLIT[a], part))
-        total = at[...].astype(F32)
-        for k in kinds:
-            total = total + back_place(a, k)[...].astype(F32)
-        return at, total
-
-    def b_merge(a, *kinds):
-        at, total = b_add(a, *kinds)
-        at[...] = total.astype(BF16)
-
-    def back1(a):
-        b_send(a, 7, 5, 6)
-
-    def back2(a):
-        b_merge(a, 7)
-        b_send(a, 3, 4)
-        b_merge(a, 5, 6)
-        b_send(a, 2)
-
-    def back3(a):
-        b_merge(a, 3)
-        b_send(a, 0)
-        b_merge(a, 4)
-        b_send(a, 1)
-
-    def back4(a):
-        _, total = b_add(a, 0, 1, 2)
-        result[a][...] = total
-
-    def to_in(which, send, recv, mine_ref, term):
-        for b in range(2):
-            rows = slice(b * 256, (b + 1) * 256)
-            own0[:, :768] = term(rows)
-            send[rows, :] = own0[:, :768].astype(BF16)
-
-            @pl.when(place.i // 4 == b)
-            def _():
-                mine_ref[...] = own0[pl.ds(pl.multiple_of((place.i % 4) * 64, 64), 64), :768]
-
-        zsum_send(which, send, recv)
-
-    out_relay(2, act)
     out_wait(1, att)
     weight_product(1)
     back1(1)
-    out_wait(2, act)
-    weight_product(3)
-    back1(3)
-    out_relay(4, qg)
+    back2(3)
+    to_in(2, zsend0, zin0, zown0, lambda r: dot(att[r, :], go[...]) + dot(act[r, :], gd[...]))
     reduce_far(3)
 
     @pl.loop(0, 3)
@@ -576,34 +607,38 @@
 
     out_send(3, bg)
     back2(1)
-    to_in(2, zsend0, zin0, zown0, lambda r: dot(att[r, :], go[...]) + dot(act[r, :], gd[...]))
+    out_relay(4, qg)
     out_wait(4, qg)
     weight_product(0)
     back1(0)
-    back2(3)
+    back3(3)
+    for b in range(2):
+        rows = slice(b * 256, (b + 1) * 256)
+        away2[:, b * 768 : (b + 1) * 768] = sum(
+            dot_nt(qg[rows, part * 384 : (part + 1) * 384], gq[part]) for part in range(3)
+        )
+    back2(0)
     out_relay(3, bg)
-    back3(1)
     out_wait(3, bg)
     weight_product(2)
     back1(2)
-    back2(0)
-    back3(3)
-
-    def input_term(r):
-        total = dot_nt(bg[r, :], gu[...])
-        for part in range(3):
-            total = total + dot_nt(qg[r, part * 384 : (part + 1) * 384], gq[part])
-        return total
-
-    to_in(3, zsend1, zin1, zown1, input_term)
+    for b in range(2):
+        rows = slice(b * 256, (b + 1) * 256)
+        away2[:, b * 768 : (b + 1) * 768] += dot_nt(bg[rows, :], gu[...])
+    ring_step(0)
+    back3(1)
+    back3(0)
+    ring_step(1)
     back2(2)
-    back3(0)
+    ring_step(2)
     hd_out[...] = fan_total("in", place.i, 8, hz_out, hz_in, vs.at[0], vr.at[0])
     fan_send("dep", place.d, 8, hd_out, hd_in, vs.at[1], vr.at[1])
     lo_buf[...] = (tok[...].astype(F32) + zsum_total(2, zsend0, zin0, zown0)).astype(BF16)
     swap_start(2, lo_buf, lo_in, layer_out)
-
-    input_grad = zsum_total(3, zsend1, zin1, zown1)
+    ring_step(3)
+    back3(2)
+
+    input_grad = ring_total()
     scaled = input_grad * gain[...]
     first = jnp.sum(scaled, axis=1, keepdims=True)
     second = jnp.sum(scaled * normed[...], axis=1, keepdims=True)
@@ -611,7 +646,8 @@
     fan_send("out", place.o, 4, tot_out, tot_in, ss.at[1], sr.at[1])
     vz_out[...] = jnp.sum(input_grad * normed[...], axis=0, keepdims=True)
     fan_send("in", place.i, 8, vz_out, vz_in, vs.at[2], vr.at[2])
-    back3(2)
+    back4(1)
+    back4(3)
     totals = fan_total("out", place.o, 4, tot_out, tot_in, ss.at[1], sr.at[1])
     centred = scaled - totals[:, :1] * (1.0 / 3072.0) - normed[...] * (totals[:, 64:65] * (1.0 / 3072.0))
     tg_buf[...] = (ups[...].astype(F32) + inverse[:, :1] * centred).astype(BF16)
@@ -620,10 +656,8 @@
     fan_send("dep", place.d, 8, vd_out, vd_in, vs.at[3], vr.at[3])
     ho_out[...] = fan_total("dep", place.d, 8, hd_out, hd_in, vs.at[1], vr.at[1])
     fan_send("out", place.o, 4, ho_out, ho_in, ss.at[2], sr.at[2])
-    back4(1)
-    back4(3)
+    back4(0)
     back4(2)
-    back4(0)
     head_grad[...] = fan_total("out", place.o, 4, ho_out, ho_in, ss.at[2], sr.at[2])[:2]
     swap_end(2, lo_buf, lo_in, layer_out)
     swap_end(3, tg_buf, tg_in, token_grad)
@@ -652,14 +686,14 @@
     scratch += [VMEM((512, 768), F32), VMEM((2, 128, 768), F32), VMEM((128, 768), BF16), VMEM((128, 768), BF16)]
     scratch += [VMEM((64, 768), BF16)] * 2 + [VMEM((768, 512), BF16)] + [VMEM((64, 768), BF16)] * 4
     scratch += full + [VMEM((7, 3, 96, 384), BF16)] + [VMEM((7, rows, cols), BF16) for rows, cols in SHARD[1:]]
-    scratch += [VMEM((512, 768), BF16)] * 2 + [VMEM((7, 64, 768), BF16)] * 2 + [VMEM((64, 768), F32)] * 2
+    scratch += [VMEM((512, 768), BF16), VMEM((7, 64, 768), BF16), VMEM((64, 768), F32)] + [VMEM((2, 4, 64, 768), BF16)] * 2
     scratch += [VMEM((64, 128), F32), VMEM((3, 64, 128), F32)]
     scratch += [VMEM((1, 768), F32), VMEM((7, 1, 768), F32)] * 2
     scratch += [VMEM((8, 128), F32), VMEM((7, 8, 128), F32)] * 2
     scratch += [VMEM((8, 128), F32), VMEM((3, 8, 128), F32)]
     dma = pltpu.SemaphoreType.DMA
     scratch += [dma((4, 8)), dma((4, 8)), dma((4,)), dma((4, 8)), dma((4, 8)), dma((3, 3)), dma((3, 3))]
-    scratch += [dma((4,)), dma((4,)), dma((5,)), dma((5,)), dma((5, 3)), dma((5, 3)), dma((3,)), dma((3,))]
+    scratch += [dma((4, 2)), dma((4, 2)), dma((5,)), dma((5,)), dma((5, 3)), dma((5, 3)), dma((3,)), dma((3,))]
     scratch += [dma((4, 8)), dma((4, 8)), dma((4, 7)), dma((4, 7)), dma((4,)), dma((4,))]
     return pl.pallas_call(
         layer_kernel,
@@ -672,11 +706,32 @@
     )(tokens, gain, head_gain, upstream, wq, wo, wu, wd)
 
 
+def settle_kernel(*refs):
+    sources, targets, sems = refs[:8], refs[8:16], refs[16]
+    copies = [pltpu.make_async_copy(a, b, sems.at[k]) for k, (a, b) in enumerate(zip(sources, targets))]
+    for copy in copies:
+        copy.start()
+    for copy in copies:
+        copy.wait()
+
+
+def settle(*arrays):
+    anywhere = pl.BlockSpec(memory_space=pl.ANY)
+    return pl.pallas_call(
+        settle_kernel,
+        out_shape=[jax.ShapeDtypeStruct(a.shape, a.dtype) for a in arrays],
+        in_specs=[anywhere] * 8,
+        out_specs=[anywhere] * 8,
+        scratch_shapes=[pltpu.SemaphoreType.DMA((8,))],
+        cost_estimate=pl.CostEstimate(flops=0, bytes_accessed=8 * 10**6, transcendentals=0),
+    )(*arrays)
+
+
 def body(tokens, norm_gain, qkv_weight, head_gain, out_weight, up_weight, down_weight, upstream):
-    layer_out, token_grad, gain_grad, head_grad, dq, do, du, dd = layer(
+    layer_out, token_grad, gain_grad, head_grad, dq, do, du, dd = settle(*layer(
         tokens[0], norm_gain[None], head_gain, upstream[0],
         jnp.transpose(qkv_weight, (1, 0, 2)), out_weight, up_weight, down_weight,
-    )
+    ))
     return (
         layer_out[None], token_grad[None], gain_grad[0], head_grad,
         jnp.transpose(dq, (1, 0, 2)), do, du, dd,

time: 172 us -> 215 us (1.25)
  Pallas kernels: 161 us -> 212 us
  local copies, waits for them, and re-layouts: 9.38 us -> 1.94 us
    pallas_call x0 -> x1, Pallas kernels: none -> 60.9 us  [settle(): pl.pallas_call(settle_kernel, out_shape=[jax.ShapeDtypeStruct(a.shape, a....]
    pallas_call x1, Pallas kernels: 161 us -> 151 us  [layer(): pl.pallas_call(layer_kernel, out_shape=outs, in_specs=[whole] * 4 + [pl.B...]
    unnamed x19 -> x4, local copies, waits for them, and re-layouts: 8.11 us -> 1.36 us
where the time goes in v2:
time: 215 us
  Pallas kernels  212 us (99%)
    pallas_call x1, Pallas kernels, layer(): pl.pallas_call(layer_kernel, out_shape=outs, in_specs=[whole] * 4 + [pl.B...  151 us
    pallas_call x1, Pallas kernels, settle(): pl.pallas_call(settle_kernel, out_shape=[jax.ShapeDtypeStruct(a.shape, a....  60.9 us

profile of v2, /device:TPU:1, one launch (start us, length us, event | category | flops | bytes accessed | tf_op | source)
XLA Modules:
  0.0 215.1 jit_solution(12099666299388330999)
XLA Ops:
  0.6 0.0 copy-start
  0.6 0.7 copy-done
  1.3 0.6 broadcast_in_dim.9.gain
  1.9 151.0 %shard_map.143 = (bf16[64,768]{1,0:T(8,128)(2,1)}, bf16[64,768]{1,0:T(8,128)(2,1)}, f32[1,768]{1,0:T(1,128)}, f32[2,128]{1,0:T(2,128)}, f32[3,96,384]{2,1,0:T(8,...) custom-call(bf16[64,768]{1,0:T(8,128)(2,1)} %bitcast.8, f32[1,768]{1,0:T(1,128)} %broadcast_in_dim.9.gain, ...), custom_call_target="tpu_custom_call" | custom-call | flops 11000000512 | bytes 10000000 | tf_op jit(solution)/shard_map/pallas_call | solution.py:698
  152.9 60.9 %shard_map.144 = (bf16[64,768]{1,0:T(8,128)(2,1)}, bf16[64,768]{1,0:T(8,128)(2,1)}, f32[1,768]{1,0:T(1,128)}, f32[2,128]{1,0:T(2,128)}, f32[3,96,384]{2,1,0:T(8,...) custom-call(bf16[64,768]{1,0:T(8,128)(2,1)} %get-tuple-element.24.refs_0_, ...), custom_call_target="tpu_custom_call" | custom-call | bytes 8000000 | tf_op jit(solution)/shard_map/pallas_call | solution.py:720
  213.8 0.0 copy-start.1
  213.8 0.7 copy-done.1
  214.5 0.6 reduce
Async XLA Ops:
  0.6 0.7 copy-start
  213.8 0.7 copy-start.1

commit v3 on v2

--- a/solution.py
+++ b/solution.py
@@ -707,11 +707,15 @@
 
 
 def settle_kernel(*refs):
-    sources, targets, sems = refs[:8], refs[8:16], refs[16]
-    copies = [pltpu.make_async_copy(a, b, sems.at[k]) for k, (a, b) in enumerate(zip(sources, targets))]
-    for copy in copies:
+    sources, targets, stages, sems = refs[:8], refs[8:16], refs[16:24], refs[24]
+    loads = [pltpu.make_async_copy(a, b, sems.at[0, k]) for k, (a, b) in enumerate(zip(sources, stages))]
+    stores = [pltpu.make_async_copy(a, b, sems.at[1, k]) for k, (a, b) in enumerate(zip(stages, targets))]
+    for copy in loads:
         copy.start()
-    for copy in copies:
+    for load, store in zip(loads, stores):
+        load.wait()
+        store.start()
+    for copy in stores:
         copy.wait()
 
 
@@ -722,7 +726,8 @@
         out_shape=[jax.ShapeDtypeStruct(a.shape, a.dtype) for a in arrays],
         in_specs=[anywhere] * 8,
         out_specs=[anywhere] * 8,
-        scratch_shapes=[pltpu.SemaphoreType.DMA((8,))],
+        scratch_shapes=[VMEM(a.shape, a.dtype) for a in arrays] + [pltpu.SemaphoreType.DMA((2, 8))],
+        compiler_params=pltpu.CompilerParams(vmem_limit_bytes=60 * 2**20),
         cost_estimate=pl.CostEstimate(flops=0, bytes_accessed=8 * 10**6, transcendentals=0),
     )(*arrays)
 

time: 215 us -> 157 us (0.73)
  Pallas kernels: 212 us -> 154 us
    pallas_call x1, Pallas kernels: 60.9 us -> 2.51 us  [settle(): pl.pallas_call(settle_kernel, out_shape=[jax.ShapeDtypeStruct(a.shape, a....]
where the time goes in v3:
time: 157 us
  Pallas kernels  154 us (98%)
  local copies, waits for them, and re-layouts  1.94 us (1%)
    pallas_call x1, Pallas kernels, layer(): pl.pallas_call(layer_kernel, out_shape=outs, in_specs=[whole] * 4 + [pl.B...  151 us

profile of v3, /device:TPU:1, one launch (start us, length us, event | category | flops | bytes accessed | tf_op | source)
XLA Modules:
  0.0 156.8 jit_solution(1600161996171837456)
XLA Ops:
  0.6 0.0 copy-start
  0.6 0.7 copy-done
  1.3 0.6 broadcast_in_dim.9.gain
  1.9 151.0 %shard_map.143 = (bf16[64,768]{1,0:T(8,128)(2,1)}, bf16[64,768]{1,0:T(8,128)(2,1)}, f32[1,768]{1,0:T(1,128)}, f32[2,128]{1,0:T(2,128)}, f32[3,96,384]{2,1,0:T(8,...) custom-call(bf16[64,768]{1,0:T(8,128)(2,1)} %bitcast.8, f32[1,768]{1,0:T(1,128)} %broadcast_in_dim.9.gain, ...), custom_call_target="tpu_custom_call" | custom-call | flops 11000000512 | bytes 10000000 | tf_op jit(solution)/shard_map/pallas_call | solution.py:698
  152.9 2.5 %shard_map.144 = (bf16[64,768]{1,0:T(8,128)(2,1)}, bf16[64,768]{1,0:T(8,128)(2,1)}, f32[1,768]{1,0:T(1,128)}, f32[2,128]{1,0:T(2,128)}, f32[3,96,384]{2,1,0:T(8,...) custom-call(bf16[64,768]{1,0:T(8,128)(2,1)} %get-tuple-element.24.refs_0_, ...), custom_call_target="tpu_custom_call" | custom-call | bytes 8000000 | tf_op jit(solution)/shard_map/pallas_call | solution.py:724
  155.5 0.0 copy-start.1
  155.5 0.7 copy-done.1
  156.2 0.6 reduce
Async XLA Ops:
  0.6 0.7 copy-start
  155.5 0.7 copy-start.1

commit v4 on v3

v4 whole, which is shorter than its diff:
```python
import math

import jax
import jax.numpy as jnp
from jax import lax
from jax.experimental import pallas as pl
from jax.experimental.pallas import tpu as pltpu
from jax.sharding import PartitionSpec as P

MESH = pl.DeviceIdType.MESH
EPSILON = 1e-06
ROOT_HALF = 1.0 / math.sqrt(2.0)
ROOT_TWO_PI = math.sqrt(2.0 * math.pi)
SCALE = 128.0 ** (-0.5)
F32 = jnp.float32
BF16 = jnp.bfloat16
VMEM = pltpu.VMEM

TILES = (384, 384, 512, 512)
COLS = (1152, 384, 1536, 1536)
SHARD = ((96, 1152), (48, 768), (96, 1536), (192, 768))
SPLIT = (48, 32, 48, 96)
BACK_ROWS = (96, 48, 96, 192, 96)
BACK_SPLIT = (48, 32, 48, 96, 48)
RING = (1, 7, 2, 6, 3, 5, 4)


def remote(src, dst, send, recv, device):
    return pltpu.make_async_remote_copy(
        src_ref=src, dst_ref=dst, send_sem=send, recv_sem=recv, device_id=device, device_id_type=MESH
    )


class Place:
    def __init__(self):
        self.i = lax.axis_index("in")
        self.o = lax.axis_index("out")
        self.d = lax.axis_index("dep")
        d = self.d
        x, y = d // 2, d % 2
        right, left, far = (x + 1) % 4, (x + 3) % 4, (x + 2) % 4
        self.me = d
        self.r, self.l, self.f = right * 2 + y, left * 2 + y, far * 2 + y
        self.p = x * 2 + 1 - y
        self.rp, self.lp, self.fp = right * 2 + 1 - y, left * 2 + 1 - y, far * 2 + 1 - y
        self.h, self.c = self.o // 2, self.o % 2
        self.mate = self.h * 2 + 1 - self.c
        self.cross = (1 - self.h) * 2 + self.c
        self.mate_at = {"out": self.mate}
        self.cross_at = {"out": self.cross, "dep": self.p}
        self.diag_at = {"out": (1 - self.h) * 2 + 1 - self.c, "dep": self.p}
        self.diag = (1 - self.h) * 2 + 1 - self.c
        self.table = (
            (self.r, self.l, self.me, self.l, "all"),
            (self.l, self.r, self.me, self.r, "all"),
            (self.p, self.p, self.me, self.p, "all"),
            (self.r, self.l, self.l, self.f, "low"),
            (self.l, self.r, self.r, self.f, "high"),
            (self.r, self.l, self.p, self.lp, "all"),
            (self.l, self.r, self.p, self.rp, "all"),
            (self.p, self.p, self.f, self.fp, "all"),
        )


def rows_of(slot, rows, split, part):
    start = slot * rows
    if part == "all":
        return pl.ds(pl.multiple_of(start, 16), rows)
    if part == "low":
        return pl.ds(pl.multiple_of(start, 16), split)
    return pl.ds(pl.multiple_of(start + split, 16), rows - split)


def greet(place):
    barrier = pltpu.get_barrier_semaphore()
    for k in range(1, 8):
        pl.semaphore_signal(barrier, inc=1, device_id={"in": (place.i + k) % 8}, device_id_type=MESH)
        pl.semaphore_signal(barrier, inc=1, device_id={"dep": (place.d + k) % 8}, device_id_type=MESH)
    for peer in (place.mate_at, place.cross_at, place.diag_at):
        pl.semaphore_signal(barrier, inc=1, device_id=peer, device_id_type=MESH)
    pl.semaphore_wait(barrier, 17)


def dot(a, b):
    return lax.dot_general(a, b, (((1,), (0,)), ((), ())), preferred_element_type=F32)


def dot_nt(a, b):
    return lax.dot_general(a, b, (((1,), (1,)), ((), ())), preferred_element_type=F32)


def dot_tn(a, b):
    return lax.dot_general(a, b, (((0,), (0,)), ((), ())), preferred_element_type=F32)


def normalize(values):
    average = jnp.mean(values, axis=-1, keepdims=True)
    spread = jnp.mean(values * values, axis=-1, keepdims=True) - average * average
    inverse = lax.rsqrt(spread + EPSILON)
    return ((values - average) * inverse, inverse)


def normalize_back(incoming, normed, inverse):
    first = jnp.mean(incoming, axis=-1, keepdims=True)
    second = jnp.mean(incoming * normed, axis=-1, keepdims=True)
    return inverse * (incoming - first - normed * second)


def layer_kernel(
    tokens, gain, head_gain, upstream, wq, wo, wu, wd,
    layer_out, token_grad, gain_grad, head_grad, dq, do, du, dd,
    gq, go, gu, gd, hid, grad, normed, inverse, fq, fo, fu,
    stat_out, stat_in, away0, away1, away2, away3, home0, home1, home2, home3, in0, in1, in2, in3,
    xs_f, xs_q, xs_o, xs_u, xs_d, xs_e, xr_f, xr_q, xr_o, xr_u, xr_d, xr_e,
    kv, att, act, bg0, bg1, qg, qlow, alow, hats, invs, kvpart, kvin, kvs, kvr,
    tok, ups, hid_t, lo_buf, lo_in, tg_buf, tg_in,
    pq, po, pu, pd, pv, rq, ro, ru, rd, rv, ring_out, ring_in,
    tot_out, tot_in, vz_out, vz_in, vd_out, vd_in, hz_out, hz_in, hd_out, hd_in, ho_out, ho_in,
    gs, gr, gl, zs, zr, ss, sr, ms, mr, cs, cr, bs, br, ks, kr, ws, wr, vs, vr, es, er,
):
    place = Place()
    bg = (bg0, bg1)
    shards = (wq, wo, wu, wd)
    gathered = (gq, go, gu, gd)
    away, home, arrived, final = (away0, away1, away2, away3), (home0, home1, home2, home3), (in0, in1, in2, in3), (fq, fo, fu)
    partial, returned = (pq, po, pu, pd, pv), (rq, ro, ru, rd, rv)
    result = (dq, do, du.at[:, :768], dd, du.at[:, 768:])
    greet(place)
    pending = []

    def start(copy):
        copy.start()
        pending.append(copy)

    def local(src, dst, sem):
        copy = pltpu.make_async_copy(src, dst, sem)
        copy.start()
        return copy

    def slots(a, ref, rows):
        return ref.at[:, rows] if a == 0 else ref.at[rows]

    def gather_copy(a, k, receive=False):
        rows, _ = SHARD[a]
        target, _, mine, theirs, part = place.table[k]
        ref = slots(a, gathered[a], rows_of(theirs if receive else mine, rows, SPLIT[a], part))
        source = ref if receive or k > 2 else shards[a]
        return remote(source, ref, gs.at[a, k], gr.at[a, k], {"dep": target})

    def g_send(a, *kinds):
        for k in kinds:
            start(gather_copy(a, k))

    def g_wait(a, *kinds):
        for k in kinds:
            gather_copy(a, k, True).wait_recv()

    own_copies = [None] * 4

    def stage1(a):
        g_send(a, 0, 1, 2)
        rows, _ = SHARD[a]
        own_copies[a] = local(shards[a], slots(a, gathered[a], rows_of(place.me, rows, 0, "all")), gl.at[a])

    def pass_left(a):
        g_wait(a, 0)
        g_send(a, 3)

    def pass_right(a):
        g_wait(a, 1)
        g_send(a, 4)

    def pass_pair(a):
        g_wait(a, 2)
        g_send(a, 5, 6)

    def stage3(a):
        g_wait(a, 3, 4)
        g_send(a, 7)

    def stage4(a):
        g_wait(a, 5, 6, 7)
        own_copies[a].wait()

    def z_slot(ref, index):
        return ref.at[pl.ds(pl.multiple_of(index * 64, 64), 64)]

    def z_ring_copy(which, kind, ref, receive=False):
        turn = kind % 4
        if kind < 4:
            target, slot = (place.i + 1) % 8, (place.i + (7 if receive else 8) - turn) % 8
        else:
            target, slot = (place.i + 7) % 8, (place.i + (1 if receive else 0) + turn) % 8
        first = 32 if kind == 7 else 0
        at = ref.at[pl.ds(pl.multiple_of(slot * 64 + first, 32), 32 if turn == 3 else 64)]
        return remote(at, at, zs.at[which, kind], zr.at[which, kind], {"in": target})

    def z_round(which, ref, turn):
        for way in (0, 4):
            if turn > 0:
                z_ring_copy(which, way + turn - 1, ref, True).wait_recv()
            start(z_ring_copy(which, way + turn, ref))

    complete = set()

    def z_done(which, ref):
        if ("z", which) not in complete:
            complete.add(("z", which))
            for way in (0, 4):
                z_ring_copy(which, way + 3, ref, True).wait_recv()

    def fan_copy(axis, index, size, k, send, recv, sem_s, sem_r):
        if axis == "out":
            peer = (place.mate_at, place.cross_at, place.diag_at)[k - 1]
        else:
            peer = {axis: (index + k) % size}
        return remote(send, recv.at[k - 1], sem_s.at[k - 1], sem_r.at[k - 1], peer)

    def fan_send(axis, index, size, send, recv, sem_s, sem_r):
        for k in range(1, size):
            start(fan_copy(axis, index, size, k, send, recv, sem_s, sem_r))

    def fan_total(axis, index, size, send, recv, sem_s, sem_r):
        total = send[...]
        for k in range(1, size):
            fan_copy(axis, index, size, k, send, recv, sem_s, sem_r).wait_recv()
            total = total + recv[k - 1]
        return total

    def out_rows(ref, index):
        return ref.at[pl.ds(pl.multiple_of(index * 128, 128), 128)]

    def out_copy(which, k, ref, receive=False):
        sent = (place.o, place.o, place.cross)[k]
        got = (place.mate, place.cross, place.diag)[k]
        target = (place.mate_at, place.cross_at, place.mate_at)[k]
        rows = out_rows(ref, got if receive else sent)
        return remote(rows, rows, bs.at[which, k], br.at[which, k], target)

    def out_send(which, ref):
        start(out_copy(which, 1, ref))
        start(out_copy(which, 0, ref))

    def out_relay(which, ref):
        out_copy(which, 1, ref, True).wait_recv()
        start(out_copy(which, 2, ref))

    def out_wait(which, ref):
        if ("out", which) not in complete:
            complete.add(("out", which))
            out_copy(which, 0, ref, True).wait_recv()
            out_copy(which, 2, ref, True).wait_recv()

    def swap_copy(k, source, landing):
        return remote(source, landing, es.at[k], er.at[k], {"dep": place.p})

    def swap_start(k, source, landing, result):
        @pl.when(place.h == 1)
        def _():
            swap_copy(k, source, landing).start()

        @pl.when(place.h == 0)
        def _():
            result[...] = source[...]

    def swap_end(k, source, landing, result):
        @pl.when(place.h == 1)
        def _():
            swap_copy(k, source, landing).wait()
            if result is not landing:
                result[...] = landing[...]

    swap_start(0, tokens, tok, tok)
    swap_start(1, upstream, ups, ups)
    lane = lax.broadcasted_iota(jnp.int32, (64, 128), 1)

    def statistics():
        swap_end(0, tokens, tok, tok)
        wide = tok[...].astype(F32)
        total = jnp.sum(wide, axis=1, keepdims=True)
        square = jnp.sum(wide * wide, axis=1, keepdims=True)
        stat_out[...] = jnp.where(lane < 64, total, square)
        fan_send("out", place.o, 4, stat_out, stat_in, ss.at[0], sr.at[0])
        swap_end(1, upstream, ups, ups)
        z_slot(grad, place.i)[...] = ups[...]
        stats = fan_total("out", place.o, 4, stat_out, stat_in, ss.at[0], sr.at[0])
        average = stats[:, :1] * (1.0 / 3072.0)
        spread = stats[:, 64:65] * (1.0 / 3072.0) - average * average
        inv = lax.rsqrt(spread + EPSILON)
        norm = (wide - average) * inv
        normed[...] = norm
        inverse[...] = jnp.broadcast_to(inv, (64, 128))
        z_slot(hid, place.i)[...] = (norm * gain[...]).astype(BF16)

    def product(a, half, out):
        left = (hid if a in (0, 2) else grad)[pl.ds(pl.multiple_of(half * 256, 256), 256), :]
        tile = TILES[a]

        @pl.loop(0, COLS[a] // tile)
        def _(t):
            cols = pl.ds(pl.multiple_of(t * tile, 128), tile)
            if a == 0:
                out[:, cols] = dot(left, gathered[a][t])
            elif a == 2:
                out[:, cols] = dot(left, gathered[a][:, cols])
            else:
                out[:, cols] = dot_nt(left, gathered[a][cols, :])

    theirs = pl.ds(pl.multiple_of((1 - place.c) * 128, 128), 128)
    ours = pl.ds(pl.multiple_of(place.c * 128, 128), 128)

    def mate_copy(a, k):
        return remote(
            (away, home)[k][a].at[theirs], arrived[a].at[pl.ds(k * 128, 128)], ms.at[a, k], mr.at[a, k], place.mate_at
        )

    far_parts = (
        ((xs_f, xr_f, 0, 0, 768), (xs_q, xr_q, 1, 768, 384)),
        ((xs_o, xr_o, 2, 0, 384),),
        ((xs_u, xr_u, 3, 0, 1536),),
        ((xs_d, xr_d, 4, 0, 768), (xs_e, xr_e, 5, 768, 768)),
    )

    def cross_copy(send, recv, k):
        return remote(send, recv, cs.at[k], cr.at[k], place.cross_at)

    def depart(a):
        stage4(a)
        z_done(*((0, hid) if a in (0, 2) else (1, grad)))
        product(a, 1 - place.h, away[a])
        mate_copy(a, 0).start()

    def remain(a):
        product(a, place.h, home[a])
        mate_copy(a, 1).start()

    def reduce_near(a):
        mate_copy(a, 0).wait_recv()
        for send, recv, k, first, count in far_parts[a]:
            cols = slice(first, first + count)
            send[...] = (away[a][ours, cols] + arrived[a][:128, cols]).astype(send.dtype)
            start(cross_copy(send, recv, k))

    def home_wait(a):
        if ("home", a) not in complete:
            complete.add(("home", a))
            mate_copy(a, 1).wait_recv()
            for k in range(2):
                mate_copy(a, k).wait_send()

    def far_sum(a, part):
        send, recv, k, first, count = far_parts[a][part]
        cols = slice(first, first + count)
        cross_copy(send, recv, k).wait_recv()
        return cols, home[a][ours, cols] + arrived[a][128:, cols] + recv[...].astype(F32)

    def reduce_far(a):
        home_wait(a)
        for part in range(len(far_parts[a])):
            cols, total = far_sum(a, part)
            final[a][:, cols] = total

    def transpose_hidden():
        z_done(0, hid)
        hid_t[...] = hid[...].T

    mine = pl.ds(pl.multiple_of(place.o * 128, 128), 128)

    def heads():
        for j in range(3):
            cols = slice(j * 128, (j + 1) * 128)
            for part in range(2):
                at = slice(part * 384 + j * 128, part * 384 + (j + 1) * 128)
                hat, hat_inv = normalize(fq[:, at])
                hats[:, at] = hat
                invs[:, at] = jnp.broadcast_to(hat_inv, (128, 128))
                low = (hat * head_gain[part : part + 1, :]).astype(BF16)
                if part == 0:
                    qlow[:, cols] = low
                else:
                    kv[mine, cols] = low
        kv[mine, 384:768] = fq[:, 768:1152].astype(BF16)
        out_send(0, kv)

    gains = []

    def attend(j):
        if j == 0:
            out_wait(0, kv)
            alow[...] = fo[...].astype(BF16)
        cols = slice(j * 128, (j + 1) * 128)
        vals = slice(384 + j * 128, 384 + (j + 1) * 128)
        query, incoming = qlow[:, cols], alow[:, cols]
        keys, values = kv[:, cols], kv[:, vals]
        scores = dot_nt(query, keys) * SCALE
        raised = jnp.exp(scores - jnp.max(scores, axis=-1, keepdims=True))
        weights = raised / jnp.sum(raised, axis=-1, keepdims=True)
        weights_low = weights.astype(BF16)
        att[mine, cols] = dot(weights_low, values).astype(BF16)
        slopes = dot_nt(incoming, values)
        centre = jnp.sum(weights * slopes, axis=-1, keepdims=True)
        score_grad = (weights * (slopes - centre)).astype(BF16)
        kvpart[:, cols] = dot_tn(score_grad, query) * SCALE
        kvpart[:, vals] = dot_tn(weights_low, incoming)
        query_grad = dot(score_grad, keys) * SCALE
        hat = hats[:, cols]
        gain_part = jnp.sum(query_grad * hat, axis=0, keepdims=True)
        back = normalize_back(query_grad * head_gain[0:1, :], hat, invs[:, cols])
        qg[mine, cols] = back.astype(BF16)
        gains.append(gain_part)

    def kv_near(h):
        rows = pl.ds(pl.multiple_of(h * 256 + (1 - place.c) * 128, 128), 128)
        return remote(kvpart.at[rows], kvin.at[h], ks.at[h], kr.at[h], place.mate_at)

    kv_far = remote(kvs, kvr, ks.at[2], kr.at[2], place.cross_at)
    def before_tile(t):
        cols = pl.ds(pl.multiple_of(t * 512, 512), 512)
        before = fu[:, cols]
        return cols, before, 0.5 * (1.0 + lax.erf(before * ROOT_HALF))

    def attend_send():
        for h in range(2):
            start(kv_near(h))
        out_send(1, att)

    def kv_across():
        for h in range(2):
            kv_near(h).wait_recv()
        other = pl.ds(pl.multiple_of(place.cross * 128, 128), 128)
        kvs[...] = (kvpart[other, :] + kvin[1 - place.h]).astype(kvs.dtype)
        start(kv_far)

    def activate():
        @pl.loop(0, 3)
        def _(t):
            cols, before, below = before_tile(t)
            act[mine, cols] = (before * below).astype(BF16)
            fu[:, cols] = below + before * jnp.exp(-0.5 * before * before) / ROOT_TWO_PI

        out_send(2, act)

    def before_back(part):
        home_wait(3)
        cols, total = far_sum(3, part)
        bg[part][mine, :] = (total * fu[:, cols]).astype(BF16)
        out_send((3, 5)[part], bg[part])

    def keys_back():
        kv_far.wait_recv()
        key_gain = jnp.zeros((1, 128), F32)
        for j in range(3):
            cols = slice(j * 128, (j + 1) * 128)
            keys = slice(384 + j * 128, 384 + (j + 1) * 128)
            vals = slice(768 + j * 128, 768 + (j + 1) * 128)
            key_grad = kvpart[mine, cols] + kvin[place.h, :, cols] + kvr[:, cols].astype(F32)
            hat = hats[:, keys]
            key_gain = key_gain + jnp.sum(key_grad * hat, axis=0, keepdims=True)
            back = normalize_back(key_grad * head_gain[1:2, :], hat, invs[:, keys])
            qg[mine, keys] = back.astype(BF16)
            value_grad = kvpart[mine, keys] + kvin[place.h, :, keys] + kvr[:, keys].astype(F32)
            qg[mine, vals] = value_grad.astype(BF16)
        out_send(4, qg)
        row = lax.broadcasted_iota(jnp.int32, (8, 128), 0)
        query_gain = gains[0] + gains[1] + gains[2]
        hz_out[...] = jnp.where(row == 0, query_gain, jnp.where(row == 1, key_gain, 0.0))
        fan_send("in", place.i, 8, hz_out, hz_in, vs.at[0], vr.at[0])

    def down_product(turn):
        if turn == 0:
            out_wait(2, act)
            z_done(1, grad)
        slot = (place.f, place.l, place.r, place.me)[turn]
        cols = pl.ds(pl.multiple_of((slot // 2) * 384, 128), 384)
        pd[cols, :] = dot_tn(act[:, cols], grad[...]).astype(BF16)
        if turn < 3:
            b_send(3, (7, 5, 6)[turn])

    def weight_product(a):
        if a == 0:
            out_wait(4, qg)

            @pl.loop(0, 3)
            def _(t):
                pq[t] = dot(hid_t[...], qg[:, pl.ds(pl.multiple_of(t * 384, 128), 384)]).astype(BF16)
        elif a == 1:
            out_wait(1, att)
            po[...] = dot_tn(att[...], grad[...]).astype(BF16)
        else:
            which, right, target = (3, bg[0], pu) if a == 2 else (5, bg[1], pv)
            out_wait(which, right)

            @pl.loop(0, 2)
            def _(t):
                cols = pl.ds(pl.multiple_of(t * 384, 128), 384)
                target[:, cols] = dot(hid_t[...], right[:, cols]).astype(BF16)

        b_send(a, 7, 5, 6)

    def back_place(a, k):
        rows = BACK_ROWS[a]
        part = place.table[k][4]
        slot = (0, 1, 2, 3, 3, 4, 5, 6)[k]
        if part == "all":
            return returned[a].at[slot]
        if part == "low":
            return slots(a, returned[a].at[slot], pl.ds(0, BACK_SPLIT[a]))
        return slots(a, returned[a].at[slot], pl.ds(BACK_SPLIT[a], rows - BACK_SPLIT[a]))

    def back_copy(a, k):
        rows = BACK_ROWS[a]
        _, target, _, slot, part = place.table[k]
        source = slots(a, partial[a], rows_of(slot, rows, BACK_SPLIT[a], part))
        return remote(source, back_place(a, k), ws.at[a, k], wr.at[a, k], {"dep": target})

    def b_send(a, *kinds):
        for k in kinds:
            start(back_copy(a, k))

    def b_add(a, *kinds):
        rows = BACK_ROWS[a]
        for k in kinds:
            back_copy(a, k).wait_recv()
        _, _, slot, _, part = place.table[kinds[0]]
        at = slots(a, partial[a], rows_of(slot, rows, BACK_SPLIT[a], part))
        total = at[...].astype(F32)
        for k in kinds:
            total = total + back_place(a, k)[...].astype(F32)
        return at, total

    def b_merge(a, *kinds):
        at, total = b_add(a, *kinds)
        at[...] = total.astype(BF16)

    def back_far(a):
        b_merge(a, 7)
        b_send(a, 3, 4)

    def back_pair(a):
        b_merge(a, 5, 6)
        b_send(a, 2)

    def back_left(a):
        b_merge(a, 3)
        b_send(a, 0)

    def back_right(a):
        b_merge(a, 4)
        b_send(a, 1)

    def back4(a):
        _, total = b_add(a, 0, 1, 2)
        result[a][...] = total

    totals_of = (home2, away2)

    def block_of(which, index):
        index = index % 8
        rows = pl.ds(pl.multiple_of((index % 4) * 64, 64), 64)
        return totals_of[which].at[rows, pl.ds(pl.multiple_of((index // 4) * 768, 128), 768)]

    def add_terms(which, term):
        for b in range(2):
            rows, cols = slice(b * 256, (b + 1) * 256), slice(b * 768, (b + 1) * 768)
            value = term(rows)
            if which in complete:
                value = totals_of[which][:, cols] + value
            totals_of[which][:, cols] = value
        complete.add(which)

    def mix():
        out_wait(1, att)
        out_wait(2, act)
        add_terms(0, lambda r: dot(att[r, :], go[...]) + dot(act[r, :], gd[...]))

    def input_heads():
        out_wait(4, qg)
        add_terms(1, lambda r: sum(dot_nt(qg[r, k * 384 : (k + 1) * 384], gq[k]) for k in range(3)))

    def input_units(part):
        which, cols = ((3, slice(0, 768)), (5, slice(768, 1536)))[part]
        out_wait(which, bg[part])
        add_terms(1, lambda r: dot_nt(bg[part][r, :], gu[:, cols]))

    def ring_copy(which, way, step):
        target = (place.i + (1, 7)[way]) % 8
        rows = (pl.ds(0, 32), pl.ds(32, 32))[way] if step == 0 else pl.ds(0, 64)
        at, k = (which, way, step, rows), way * 4 + step
        return remote(ring_out.at[at], ring_in.at[at], zs.at[2 + which, k], zr.at[2 + which, k], {"in": target})

    def ring_step(which, step):
        for way in range(2):
            block = block_of(which, place.i + (4 - step, 4 + step)[way])
            if step == 0:
                ring_out[which, way, 0] = block[...].astype(BF16)
            else:
                ring_copy(which, way, step - 1).wait_recv()
                if step == 1:
                    half = (slice(0, 32), slice(32, 64))[way]
                    block[half, :] += ring_in[which, way, 0, half, :].astype(F32)
                    ring_out[which, way, 1] = block[...].astype(BF16)
                else:
                    ring_out[which, way, step] = (block[...] + ring_in[which, way, step - 1].astype(F32)).astype(BF16)
            start(ring_copy(which, way, step))

    def ring_total(which):
        total = block_of(which, place.i)[...]
        for way in range(2):
            ring_copy(which, way, 3).wait_recv()
            total = total + ring_in[which, way, 3].astype(F32)
        return total

    def finish_layer():
        lo_buf[...] = (tok[...].astype(F32) + ring_total(0)).astype(BF16)
        swap_start(2, lo_buf, lo_in, layer_out)

    def head_in():
        hd_out[...] = fan_total("in", place.i, 8, hz_out, hz_in, vs.at[0], vr.at[0])
        fan_send("dep", place.d, 8, hd_out, hd_in, vs.at[1], vr.at[1])

    def head_dep():
        ho_out[...] = fan_total("dep", place.d, 8, hd_out, hd_in, vs.at[1], vr.at[1])
        fan_send("out", place.o, 4, ho_out, ho_in, ss.at[2], sr.at[2])

    held = []

    def input_sums():
        input_grad = ring_total(1)
        scaled = input_grad * gain[...]
        held.append(scaled)
        first = jnp.sum(scaled, axis=1, keepdims=True)
        second = jnp.sum(scaled * normed[...], axis=1, keepdims=True)
        tot_out[...] = jnp.where(lane < 64, first, second)
        fan_send("out", place.o, 4, tot_out, tot_in, ss.at[1], sr.at[1])
        vz_out[...] = jnp.sum(input_grad * normed[...], axis=0, keepdims=True)
        fan_send("in", place.i, 8, vz_out, vz_in, vs.at[2], vr.at[2])

    def finish_tokens():
        totals = fan_total("out", place.o, 4, tot_out, tot_in, ss.at[1], sr.at[1])
        centred = held[0] - totals[:, :1] * (1.0 / 3072.0) - normed[...] * (totals[:, 64:65] * (1.0 / 3072.0))
        tg_buf[...] = (ups[...].astype(F32) + inverse[:, :1] * centred).astype(BF16)
        swap_start(3, tg_buf, tg_in, token_grad)

    def gain_in():
        vd_out[...] = fan_total("in", place.i, 8, vz_out, vz_in, vs.at[2], vr.at[2])
        fan_send("dep", place.d, 8, vd_out, vd_in, vs.at[3], vr.at[3])

    def finish():
        head_grad[...] = fan_total("out", place.o, 4, ho_out, ho_in, ss.at[2], sr.at[2])[:2]
        gain_grad[...] = fan_total("dep", place.d, 8, vd_out, vd_in, vs.at[3], vr.at[3])
        swap_end(2, lo_buf, lo_in, layer_out)
        swap_end(3, tg_buf, tg_in, token_grad)

    stage1(0)
    statistics()
    z_round(0, hid, 0)
    stage1(1)
    pass_left(0)
    pass_right(0)
    pass_pair(0)
    z_round(0, hid, 1)
    pass_right(1)
    stage3(0)
    stage1(2)
    z_round(0, hid, 2)
    z_round(1, grad, 0)
    pass_left(1)
    z_round(0, hid, 3)
    z_round(1, grad, 1)
    pass_pair(1)
    depart(0)
    reduce_near(0)
    pass_right(2)
    pass_left(2)
    pass_pair(2)
    transpose_hidden()
    z_round(1, grad, 2)
    stage3(1)
    z_round(1, grad, 3)
    stage3(2)
    remain(0)
    stage1(3)
    depart(1)
    reduce_near(1)
    reduce_far(0)
    heads()
    depart(2)
    reduce_near(2)
    pass_left(3)
    pass_right(3)
    remain(1)
    out_relay(0, kv)
    pass_pair(3)
    remain(2)
    reduce_far(1)
    attend(0)
    stage3(3)
    attend(1)
    reduce_far(2)
    activate()
    attend(2)
    attend_send()
    kv_across()
    depart(3)
    out_relay(2, act)
    reduce_near(3)
    down_product(0)
    down_product(1)
    down_product(2)
    out_relay(1, att)
    remain(3)
    keys_back()
    down_product(3)
    back_far(3)
    weight_product(1)
    before_back(0)
    mix()
    back_far(1)
    back_right(3)
    before_back(1)
    back_left(3)
    back_pair(3)
    out_relay(4, qg)
    ring_step(0, 0)
    back_right(1)
    back_left(1)
    back_pair(1)
    weight_product(0)
    ring_step(0, 1)
    out_relay(3, bg[0])
    input_heads()
    weight_product(2)
    out_relay(5, bg[1])
    input_units(0)
    input_units(1)
    ring_step(1, 0)
    back_far(0)
    weight_product(4)
    ring_step(1, 1)
    back_far(2)
    back_pair(0)
    back_pair(2)
    ring_step(0, 2)
    back4(1)
    back_right(0)
    ring_step(1, 2)
    back_far(4)
    back_left(0)
    ring_step(0, 3)
    back_pair(4)
    ring_step(1, 3)
    finish_layer()
    head_in()
    back_left(2)
    back_right(2)
    input_sums()
    head_dep()
    back_right(4)
    back4(0)
    back_left(4)
    finish_tokens()
    back4(3)
    back4(2)
    gain_in()
    back4(4)
    finish()
    for copy in pending:
        copy.wait_send()


def layer(tokens, gain, head_gain, upstream, wq, wo, wu, wd):
    shape = jax.ShapeDtypeStruct
    outs = [
        shape((64, 768), BF16), shape((64, 768), BF16), shape((1, 768), F32), shape((2, 128), F32),
        shape((3, 96, 384), F32), shape((48, 768), F32), shape((96, 1536), F32), shape((192, 768), F32),
    ]
    whole = pl.BlockSpec(memory_space=VMEM)
    far = [VMEM((128, 768), F32), VMEM((128, 384), BF16), VMEM((128, 384), F32), VMEM((128, 1536), BF16)]
    far += [VMEM((128, 768), BF16)] * 2
    full = [VMEM((3, 768, 384), BF16), VMEM((384, 768), BF16), VMEM((768, 1536), BF16), VMEM((1536, 768), BF16)]
    scratch = full + [VMEM((512, 768), BF16), VMEM((512, 768), BF16), VMEM((64, 768), F32), VMEM((64, 128), F32)]
    scratch += [VMEM((128, n), F32) for n in COLS[:3]]
    scratch += [VMEM((64, 128), F32), VMEM((3, 64, 128), F32)]
    for _ in range(3):
        scratch += [VMEM((256, n), F32) for n in COLS]
    scratch += far + far
    scratch += [VMEM((512, n), BF16) for n in (768, 384, 1536, 768, 768, 1152)]
    scratch += [VMEM((128, 384), BF16), VMEM((128, 384), BF16), VMEM((128, 768), F32), VMEM((128, 768), F32)]
    scratch += [VMEM((512, 768), F32), VMEM((2, 128, 768), F32), VMEM((128, 768), BF16), VMEM((128, 768), BF16)]
    scratch += [VMEM((64, 768), BF16)] * 2 + [VMEM((768, 512), BF16)] + [VMEM((64, 768), BF16)] * 4
    scratch += [VMEM((3, 768, 384), BF16), VMEM((384, 768), BF16), VMEM((768, 768), BF16), VMEM((1536, 768), BF16), VMEM((768, 768), BF16)]
    scratch += [VMEM((7, 3, 96, 384), BF16)] + [VMEM((7, rows, 768), BF16) for rows in BACK_ROWS[1:]]
    scratch += [VMEM((2, 2, 4, 64, 768), BF16)] * 2
    scratch += [VMEM((64, 128), F32), VMEM((3, 64, 128), F32)]
    scratch += [VMEM((1, 768), F32), VMEM((7, 1, 768), F32)] * 2
    scratch += [VMEM((8, 128), F32), VMEM((7, 8, 128), F32)] * 2
    scratch += [VMEM((8, 128), F32), VMEM((3, 8, 128), F32)]
    dma = pltpu.SemaphoreType.DMA
    scratch += [dma((4, 8)), dma((4, 8)), dma((4,)), dma((4, 8)), dma((4, 8)), dma((3, 3)), dma((3, 3))]
    scratch += [dma((4, 2)), dma((4, 2)), dma((6,)), dma((6,)), dma((6, 3)), dma((6, 3)), dma((3,)), dma((3,))]
    scratch += [dma((5, 8)), dma((5, 8)), dma((4, 7)), dma((4, 7)), dma((4,)), dma((4,))]
    return pl.pallas_call(
        layer_kernel,
        out_shape=outs,
        in_specs=[whole] * 4 + [pl.BlockSpec(memory_space=pl.ANY)] * 4,
        out_specs=[whole] * len(outs),
        scratch_shapes=scratch,
        compiler_params=pltpu.CompilerParams(collective_id=1, has_side_effects=True, vmem_limit_bytes=62 * 2**20),
        cost_estimate=pl.CostEstimate(flops=11 * 10**9, bytes_accessed=10**7, transcendentals=10**6),
    )(tokens, gain, head_gain, upstream, wq, wo, wu, wd)


def settle_kernel(*refs):
    sources, targets, stages, sems = refs[:8], refs[8:16], refs[16:24], refs[24]
    loads = [pltpu.make_async_copy(a, b, sems.at[0, k]) for k, (a, b) in enumerate(zip(sources, stages))]
    stores = [pltpu.make_async_copy(a, b, sems.at[1, k]) for k, (a, b) in enumerate(zip(stages, targets))]
    for copy in loads:
        copy.start()
    for load, store in zip(loads, stores):
        load.wait()
        store.start()
    for copy in stores:
        copy.wait()


def settle(*arrays):
    anywhere = pl.BlockSpec(memory_space=pl.ANY)
    return pl.pallas_call(
        settle_kernel,
        out_shape=[jax.ShapeDtypeStruct(a.shape, a.dtype) for a in arrays],
        in_specs=[anywhere] * 8,
        out_specs=[anywhere] * 8,
        scratch_shapes=[VMEM(a.shape, a.dtype) for a in arrays] + [pltpu.SemaphoreType.DMA((2, 8))],
        compiler_params=pltpu.CompilerParams(vmem_limit_bytes=60 * 2**20),
        cost_estimate=pl.CostEstimate(flops=0, bytes_accessed=8 * 10**6, transcendentals=0),
    )(*arrays)


def body(tokens, norm_gain, qkv_weight, head_gain, out_weight, up_weight, down_weight, upstream):
    layer_out, token_grad, gain_grad, head_grad, dq, do, du, dd = settle(*layer(
        tokens[0], norm_gain[None], head_gain, upstream[0],
        jnp.transpose(qkv_weight, (1, 0, 2)), out_weight, up_weight, down_weight,
    ))
    return (
        layer_out[None], token_grad[None], gain_grad[0], head_grad,
        jnp.transpose(dq, (1, 0, 2)), do, du, dd,
    )


def solution(mesh):
    placed = (
        P("dep", "in", "out"),
        P("out"),
        P(("out", "dep"), None, "in"),
        P(),
        P(("in", "dep"), "out"),
        P(("out", "dep"), "in"),
        P(("in", "dep"), "out"),
        P("dep", "in", "out"),
    )
    return jax.shard_map(
        body,
        mesh=mesh,
        in_specs=placed,
        out_specs=(
            P("dep", "in", "out"),
            P("dep", "in", "out"),
            P("out"),
            P(),
            P(("out", "dep"), None, "in"),
            P(("in", "dep"), "out"),
            P(("out", "dep"), "in"),
            P(("in", "dep"), "out"),
        ),
        check_vma=False,
    )
```

time: 157 us -> 146 us (0.930)
  Pallas kernels: 154 us -> 141 us
    pallas_call x1, Pallas kernels: 151 us -> 139 us  [layer(): pl.pallas_call(layer_kernel, out_shape=outs, in_specs=[whole] * 4 + [pl.B...]
where the time goes in v4:
time: 146 us; the launch traced here: 144 us
  Pallas kernels  141 us (97%)
  local copies, waits for them, and re-layouts  1.94 us (1%)
    pallas_call x1, Pallas kernels, layer(): pl.pallas_call(layer_kernel, out_shape=outs, in_specs=[whole] * 4 + [pl.B...  139 us

profile of v4, /device:TPU:1, one launch (start us, length us, event | category | flops | bytes accessed | tf_op | source)
XLA Modules:
  0.0 144.3 jit_solution(14263741907175243970)
XLA Ops:
  0.6 0.0 copy-start
  0.6 0.7 copy-done
  1.3 0.6 broadcast_in_dim.9.gain
  1.9 138.6 %shard_map.143 = (bf16[64,768]{1,0:T(8,128)(2,1)}, bf16[64,768]{1,0:T(8,128)(2,1)}, f32[1,768]{1,0:T(1,128)}, f32[2,128]{1,0:T(2,128)}, f32[3,96,384]{2,1,0:T(8,...) custom-call(bf16[64,768]{1,0:T(8,128)(2,1)} %bitcast.8, f32[1,768]{1,0:T(1,128)} %broadcast_in_dim.9.gain, ...), custom_call_target="tpu_custom_call" | custom-call | flops 11000000512 | bytes 10000000 | tf_op jit(solution)/shard_map/pallas_call | solution.py:802
  140.5 2.5 %shard_map.144 = (bf16[64,768]{1,0:T(8,128)(2,1)}, bf16[64,768]{1,0:T(8,128)(2,1)}, f32[1,768]{1,0:T(1,128)}, f32[2,128]{1,0:T(2,128)}, f32[3,96,384]{2,1,0:T(8,...) custom-call(bf16[64,768]{1,0:T(8,128)(2,1)} %get-tuple-element.24.refs_0_, ...), custom_call_target="tpu_custom_call" | custom-call | bytes 8000000 | tf_op jit(solution)/shard_map/pallas_call | solution.py:828
  143.0 0.0 copy-start.1
  143.0 0.7 copy-done.1
  143.7 0.6 reduce
Async XLA Ops:
  0.6 0.7 copy-start
  143.0 0.7 copy-start.1

commit v5 on v4

--- a/solution.py
+++ b/solution.py
@@ -290,7 +290,7 @@
         norm = (wide - average) * inv
         normed[...] = norm
         inverse[...] = jnp.broadcast_to(inv, (64, 128))
-        z_slot(hid, place.i)[...] = (norm * gain[...]).astype(BF16)
+        z_slot(hid, place.i)[...] = (norm * gain[...].reshape(1, 768)).astype(BF16)
 
     def product(a, half, out):
         left = (hid if a in (0, 2) else grad)[pl.ds(pl.multiple_of(half * 256, 256), 256), :]
@@ -626,7 +626,7 @@
 
     def input_sums():
         input_grad = ring_total(1)
-        scaled = input_grad * gain[...]
+        scaled = input_grad * gain[...].reshape(1, 768)
         held.append(scaled)
         first = jnp.sum(scaled, axis=1, keepdims=True)
         second = jnp.sum(scaled * normed[...], axis=1, keepdims=True)
@@ -647,7 +647,7 @@
 
     def finish():
         head_grad[...] = fan_total("out", place.o, 4, ho_out, ho_in, ss.at[2], sr.at[2])[:2]
-        gain_grad[...] = fan_total("dep", place.d, 8, vd_out, vd_in, vs.at[3], vr.at[3])
+        gain_grad[...] = fan_total("dep", place.d, 8, vd_out, vd_in, vs.at[3], vr.at[3]).reshape(768)
         swap_end(2, lo_buf, lo_in, layer_out)
         swap_end(3, tg_buf, tg_in, token_grad)
 
@@ -771,7 +771,7 @@
 def layer(tokens, gain, head_gain, upstream, wq, wo, wu, wd):
     shape = jax.ShapeDtypeStruct
     outs = [
-        shape((64, 768), BF16), shape((64, 768), BF16), shape((1, 768), F32), shape((2, 128), F32),
+        shape((64, 768), BF16), shape((64, 768), BF16), shape((768,), F32), shape((2, 128), F32),
         shape((3, 96, 384), F32), shape((48, 768), F32), shape((96, 1536), F32), shape((192, 768), F32),
     ]
     whole = pl.BlockSpec(memory_space=VMEM)
@@ -838,11 +838,11 @@
 
 def body(tokens, norm_gain, qkv_weight, head_gain, out_weight, up_weight, down_weight, upstream):
     layer_out, token_grad, gain_grad, head_grad, dq, do, du, dd = settle(*layer(
-        tokens[0], norm_gain[None], head_gain, upstream[0],
+        tokens[0], norm_gain, head_gain, upstream[0],
         jnp.transpose(qkv_weight, (1, 0, 2)), out_weight, up_weight, down_weight,
     ))
     return (
-        layer_out[None], token_grad[None], gain_grad[0], head_grad,
+        layer_out[None], token_grad[None], gain_grad, head_grad,
         jnp.transpose(dq, (1, 0, 2)), do, du, dd,
     )
 

time: 146 us -> 144 us (0.986)
  local copies, waits for them, and re-layouts: 1.94 us -> 0 us
where the time goes in v5:
time: 144 us; the launch traced here: 142 us
  Pallas kernels  141 us (98%)
    pallas_call x1, Pallas kernels, layer(): pl.pallas_call(layer_kernel, out_shape=outs, in_specs=[whole] * 4 + [pl.B...  139 us

profile of v5, /device:TPU:1, one launch (start us, length us, event | category | flops | bytes accessed | tf_op | source)
XLA Modules:
  0.0 142.0 jit_solution(2736188748510695607)
XLA Ops:
  0.6 138.7 %shard_map.143 = (bf16[64,768]{1,0:T(8,128)(2,1)}, bf16[64,768]{1,0:T(8,128)(2,1)}, f32[768]{0:T(1024)}, f32[2,128]{1,0:T(2,128)}, f32[3,96,384]{2,1,0:T(8,128)}...) custom-call(bf16[64,768]{1,0:T(8,128)(2,1)} %bitcast.8, f32[768]{0:T(1024)} %gain.1, ...), custom_call_target="tpu_custom_call" | custom-call | flops 11000000512 | bytes 10000000 | tf_op jit(solution)/shard_map/pallas_call | solution.py:802
  139.4 2.5 %shard_map.144 = (bf16[64,768]{1,0:T(8,128)(2,1)}, bf16[64,768]{1,0:T(8,128)(2,1)}, f32[768]{0:T(1024)}, f32[2,128]{1,0:T(2,128)}, f32[3,96,384]{2,1,0:T(8,128)}...) custom-call(bf16[64,768]{1,0:T(8,128)(2,1)} %get-tuple-element.24.refs_0_, ...), custom_call_target="tpu_custom_call" | custom-call | bytes 8000000 | tf_op jit(solution)/shard_map/pallas_call | solution.py:828
